TPU v7x, 32 devices: a whole 2x2x4 slice. The times are simulated.
32 devices in a mesh: lat: 4 (over y, x), lon: 8 (over z, core).
Axes of the slice: x: 2, y: 2, z: 4, core: 2. Of those that a mesh axis runs over, the one named last changes fastest.
Arguments:
- features: bfloat16 [128, 1024, 128], P('lat', 'lon'), may hold values from -6 to 6
- land_mask: int32 [128, 1024], P('lat', 'lon'), may hold values 0 or 1
- dw_weight: float32 [7, 7, 128], replicated, may hold values from -0.875 to 0.875
- dw_bias: float32 [128], replicated, may hold values from -3 to 3
- norm_gain: float32 [128], replicated, may hold values from 0.25 to 1.75
- norm_shift: float32 [128], replicated, may hold values from -3 to 3
- expand_weight: bfloat16 [128, 512], replicated, may hold values from -0.5 to 0.5
- expand_bias: float32 [512], replicated, may hold values from -3 to 3
- project_weight: bfloat16 [512, 128], replicated, may hold values from -0.25 to 0.25
- project_bias: float32 [128], replicated, may hold values from -3 to 3
- layer_scale: float32 [128], replicated, may hold values from 0.3 to 1
- out_gain: float32 [128], replicated, may hold values from 0.25 to 1.75
- out_shift: float32 [128], replicated, may hold values from -3 to 3
- coarse_weight: bfloat16 [4, 4, 128, 256], replicated, may hold values from -0.125 to 0.125
- coarse_bias: float32 [256], replicated, may hold values from -3 to 3
Outputs:
- coarse: bfloat16 [64, 512, 256], P('lat', 'lon')
All inputs are finite; a program needn't handle non-finite values. No bound on the sum of `land_mask` on one device may be relied on, other than what follows from the above.
Results may differ from a plain program's by a relative error of at most 0.0051.
Values may be sent and summed in bfloat16 or wider, within the bound.
A program may use at most 64 MiB of HBM per device.

v0:
```python
import jax
import jax.numpy as jnp
from jax import lax
from jax.sharding import PartitionSpec as P


def swapped(block, axis, apart):
    count = lax.axis_size(axis)
    route = []
    for low in range(count):
        high = low | 1 << apart
        if high != low and high < count:
            route += [(low, high), (high, low)]
    return lax.ppermute(block, axis, route)


def extended_2(cells, sides, width):
    for axis, dim in sides:
        count = lax.axis_size(axis)
        head = lax.slice_in_dim(cells, 0, width, axis=dim)
        tail = lax.slice_in_dim(cells, cells.shape[dim] - width, cells.shape[dim], axis=dim)
        cells = jnp.concatenate(
            [
                lax.ppermute(tail, axis, [(i, (i + 1) % count) for i in range(count)]),
                cells,
                lax.ppermute(head, axis, [((i + 1) % count, i) for i in range(count)]),
            ],
            axis=dim,
        )
    return cells


def layer_norm(values, gain, shift):
    center = values - jnp.mean(values, axis=-1, keepdims=True)
    spread = jnp.mean(center * center, axis=-1, keepdims=True)
    return center * lax.rsqrt(spread + 1e-06) * gain + shift


def reflect(fold_band):
    partner = fold_band
    for bit_index in range(lax.axis_size("lon").bit_length() - 1):
        partner = swapped(partner, "lon", bit_index)
    return partner[::-1, ::-1]


def extend(grid_field, rim_size):
    row_count = grid_field.shape[0]
    extended = extended_2(grid_field, (("lat", 0), ("lon", 1)), rim_size)
    fold_band = extended[row_count : row_count + rim_size]
    north_band = reflect(fold_band)
    lat_index = lax.axis_index("lat")
    top_index = lax.axis_size("lat") - 1
    south_rim = jnp.where(lat_index == 0, jnp.zeros_like(extended[:rim_size]), extended[:rim_size])
    north_rim = jnp.where(lat_index == top_index, north_band, extended[-rim_size:])
    total_rows = extended.shape[0]
    extended = extended.at[:rim_size].set(south_rim)
    return extended.at[total_rows - rim_size :].set(north_rim)


def convnext_cells(
    padded_in,
    centre,
    land_mask,
    dw_weight,
    dw_bias,
    norm_gain,
    norm_shift,
    expand_weight,
    expand_bias,
    project_weight,
    project_bias,
    layer_scale,
    out_gain,
    out_shift,
):
    height, breadth, channels = centre.shape
    spatial = jnp.zeros(centre.shape, jnp.float32) + dw_bias
    for col_tap in range(dw_weight.shape[1]):
        shifted = padded_in[:, col_tap : col_tap + breadth].astype(jnp.float32)
        for row_tap in range(dw_weight.shape[0]):
            spatial = spatial + shifted[row_tap : row_tap + height] * dw_weight[row_tap, col_tap]
    normed = layer_norm(spatial, norm_gain, norm_shift).astype(jnp.bfloat16).reshape(-1, channels)
    hidden = jax.nn.gelu(
        jnp.dot(normed, expand_weight, preferred_element_type=jnp.float32) + expand_bias,
        approximate=False,
    ).astype(jnp.bfloat16)
    updated = centre.reshape(-1, channels).astype(jnp.float32) + layer_scale * (
        jnp.dot(hidden, project_weight, preferred_element_type=jnp.float32) + project_bias
    )
    marks = land_mask.reshape(-1, 1).astype(jnp.float32)
    normalized = marks * layer_norm(updated, out_gain, out_shift)
    return normalized.astype(jnp.bfloat16).reshape(height, breadth, channels)


def shrink_cells(padded, coarse_weight, coarse_bias):
    height = padded.shape[0] - 2
    breadth = padded.shape[1] - 2
    channels = padded.shape[2]
    out_count = coarse_weight.shape[3]
    half_rows = height // 2
    half_cols = breadth // 2
    paired = padded.reshape(half_rows + 1, 2, half_cols + 1, 2 * channels)
    total = jnp.zeros((half_rows * half_cols, out_count), jnp.float32) + coarse_bias
    for col_pair in range(2):
        col_shifted = paired[:, :, col_pair : col_pair + half_cols]
        for row_pair in range(2):
            for parity in range(2):
                window = col_shifted[row_pair : row_pair + half_rows, parity].reshape(
                    -1, 2 * channels
                )
                kernel = coarse_weight[
                    2 * row_pair + parity, 2 * col_pair : 2 * col_pair + 2
                ].reshape(2 * channels, out_count)
                total = total + jnp.dot(window, kernel, preferred_element_type=jnp.float32)
    return total.astype(jnp.bfloat16).reshape(half_rows, half_cols, out_count)


def local(
    features,
    land_mask,
    dw_weight,
    dw_bias,
    norm_gain,
    norm_shift,
    expand_weight,
    expand_bias,
    project_weight,
    project_bias,
    layer_scale,
    out_gain,
    out_shift,
    coarse_weight,
    coarse_bias,
):
    padded_in = extend(features, 3)
    normalized = convnext_cells(
        padded_in,
        features,
        land_mask,
        dw_weight,
        dw_bias,
        norm_gain,
        norm_shift,
        expand_weight,
        expand_bias,
        project_weight,
        project_bias,
        layer_scale,
        out_gain,
        out_shift,
    )
    padded_out = extend(normalized, 1)
    return shrink_cells(padded_out, coarse_weight, coarse_bias)


def solution(mesh):
    placed = (
        P("lat", "lon", None),
        P("lat", "lon"),
        P(),
        P(),
        P(),
        P(),
        P(),
        P(),
        P(),
        P(),
        P(),
        P(),
        P(),
        P(),
        P(),
    )
    return jax.shard_map(
        local, mesh=mesh, in_specs=placed, out_specs=P("lat", "lon", None), check_vma=False
    )
```

profile of v0, /device:TPU:0, one launch (start us, length us, event | category | flops | bytes accessed | tf_op | source)
XLA Modules:
  0.0 136.2 jit_solution(1304441779929503751)
XLA Ops:
  0.0 1.0 fusion.103
  1.0 3.0 %collective-permute-start = (bf16[3,128,128]{2,1,0:T(8,128)(2,1)S(1)}, bf16[3,128,128]{2,1,0:T(8,128)(2,1)S(1)}, u32[]{:S(2)}, u32[]{:S(2)}) collective-permute-start(bf16[3,128,128]{2,1,0:T(8,128)(2,1)S(1)} %get-tuple-element.89), channel_id=1, source_target_pairs={{0,8},{8,16},{16,24},{24,0},{1,9},{9,17},{17,25},{25,1},{2,10},{10... | collective-permute-start | bytes 294920 | tf_op jit(solution)/shard_map/ppermute | solution.py:24
  4.0 1.0 collective-permute-start.1
  5.0 3.4 %collective-permute-done = bf16[3,128,128]{2,1,0:T(8,128)(2,1)S(1)} collective-permute-done((bf16[3,128,128]{2,1,0:T(8,128)(2,1)S(1)}, bf16[3,128,128]{2,1,0:T(8,128)(2,1)S(1)}, u32[]{:S(2)}, u32[]{:S(2)}) %collective-permute-start) | collective-permute-done | bytes 98336 | tf_op jit(solution)/shard_map/ppermute | solution.py:24
  8.5 1.4 %constant_dynamic-update-slice_fusion.1 = bf16[38,128,128]{2,1,0:T(8,128)(2,1)S(1)} fusion(bf16[38,128,128]{2,1,0:T(8,128)(2,1)S(1)} %constant_dynamic-update-slice_fusion.2, bf16[32,128,128]{2,1,0:T(8,128)(2,1)} %param.23), kind=kLoop, calls=%fused_computation.159 | loop fusion | bytes 2097152
  9.9 0.2 collective-permute-done.1
  10.2 3.5 %collective-permute-start.3 = (bf16[38,3,128]{2,1,0:T(4,128)(2,1)S(1)}, bf16[38,3,128]{2,1,0:T(4,128)(2,1)S(1)}, u32[]{:S(2)}, u32[]{:S(2)}) collective-permute-start(bf16[38,3,128]{2,1,0:T(4,128)(2,1)S(1)} %get-tuple-element.73), channel_id=1, source_target_pairs={{1,0},{2,1},{3,2},{4,3},{5,4},{6,5},{7,6},{0,7},{9,8},{10,9},{11,1... | collective-permute-start | bytes 87560 | tf_op jit(solution)/shard_map/ppermute | solution.py:26
  13.8 1.7 %collective-permute-done.2 = bf16[38,3,128]{2,1,0:T(4,128)(2,1)S(1)} collective-permute-done((bf16[38,3,128]{2,1,0:T(4,128)(2,1)S(1)}, bf16[38,3,128]{2,1,0:T(4,128)(2,1)S(1)}, u32[]{:S(2)}, u32[]{:S(2)}) %collective-permute-start.2) | collective-permute-done | bytes 29216 | tf_op jit(solution)/shard_map/ppermute | solution.py:24
  15.4 0.6 pad_maximum_fusion
  16.1 1.1 copy.18
  17.1 1.6 %fusion.98 = (bf16[3,134,128]{2,1,0:T(8,128)(2,1)S(1)}, bf16[38,134,128]{2,1,0:T(8,128)(2,1)}) fusion(bf16[38,134,128]{2,1,0:T(8,128)(2,1)} %copy.18, pred[]{:T(512)S(6)} %eq.8), kind=kLoop, calls=%fused_computation.243 | loop fusion | flops 51456 | bytes 416257 | tf_op jit(solution)/shard_map/slice | solution.py:49
  18.7 0.2 collective-permute-start.4
  19.0 1.1 collective-permute-done.4
  20.1 1.4 %collective-permute-start.5 = (bf16[3,134,128]{2,1,0:T(8,128)(2,1)S(1)}, bf16[3,134,128]{2,1,0:T(8,128)(2,1)S(1)}, u32[]{:S(2)}, u32[]{:S(2)}) collective-permute-start(bf16[3,134,128]{2,1,0:T(8,128)(2,1)S(1)} %collective-permute-done.4), channel_id=1, source_target_pairs={{0,2},{2,0},{1,3},{3,1},{4,6},{6,4},{5,7},{7,5},{8,10},{10,8},{9,1... | collective-permute-start | bytes 308744 | tf_op jit(solution)/shard_map/ppermute | solution.py:14
  21.5 3.7 %collective-permute-done.5 = bf16[3,134,128]{2,1,0:T(8,128)(2,1)S(1)} collective-permute-done((bf16[3,134,128]{2,1,0:T(8,128)(2,1)S(1)}, bf16[3,134,128]{2,1,0:T(8,128)(2,1)S(1)}, u32[]{:S(2)}, u32[]{:S(2)}) %collective-permute-start.5) | collective-permute-done | bytes 102944 | tf_op jit(solution)/shard_map/ppermute | solution.py:14
  25.1 2.5 %collective-permute-start.6 = (bf16[3,134,128]{2,1,0:T(8,128)(2,1)S(1)}, bf16[3,134,128]{2,1,0:T(8,128)(2,1)S(1)}, u32[]{:S(2)}, u32[]{:S(2)}) collective-permute-start(bf16[3,134,128]{2,1,0:T(8,128)(2,1)S(1)} %collective-permute-done.5), channel_id=1, source_target_pairs={{0,4},{4,0},{1,5},{5,1},{2,6},{6,2},{3,7},{7,3},{8,12},{12,8},{9,1... | collective-permute-start | bytes 308744 | tf_op jit(solution)/shard_map/ppermute | solution.py:14
  27.6 4.9 %collective-permute-done.6 = bf16[3,134,128]{2,1,0:T(8,128)(2,1)S(1)} collective-permute-done((bf16[3,134,128]{2,1,0:T(8,128)(2,1)S(1)}, bf16[3,134,128]{2,1,0:T(8,128)(2,1)S(1)}, u32[]{:S(2)}, u32[]{:S(2)}) %collective-permute-start.6) | collective-permute-done | bytes 102944 | tf_op jit(solution)/shard_map/ppermute | solution.py:14
  32.6 0.4 rev.6
  33.0 0.7 fusion.62
  33.7 11.2 %slice_convert_fusion.6 = (f32[38,128,128]{2,1,0:T(8,128)S(1)}, f32[38,128,128]{2,1,0:T(8,128)}, f32[38,128,128]{2,1,0:T(8,128)}, f32[38,128,128]{2,1,0:T(8,128)...) fusion(bf16[38,134,128]{2,1,0:T(8,128)(2,1)} %fusion.62), kind=kLoop, calls=%fused_computation.140 | loop fusion | flops 4358144 | bytes 26148864 | tf_op jit(solution)/shard_map/convert_element_type | solution.py:79
  44.9 33.4 %fusion.96 = (f32[32,128]{1,0:T(8,128)S(1)}, f32[32,128,128]{2,1,0:T(8,128)}) fusion(f32[128]{0:T(128)S(1)} %get-tuple-element.137, f32[38,128,128]{2,1,0:T(8,128)} %get-tuple-element.56, f32[128]{0:T(128)S(1)} %get-tuple-element.138, f32[128]{0:T(128)S(1)} %get-tuple-element.91, f32[128]{0:T(128)S(1)} %get-tuple-element.92, f32[128]{0:T(128)S(1)} %get-tuple-element.93, ...), kind=kLoop, calls=%fused_computation.242 | loop fusion | flops 51900416 | bytes 104899584 | tf_op jit(solution)/shard_map/reduce_sum | solution.py:34
  78.4 2.7 %multiply_reduce_fusion.1 = f32[32,128]{1,0:T(8,128)S(1)} fusion(f32[32,128,128]{2,1,0:T(8,128)} %get-tuple-element.54, f32[32,128]{1,0:T(8,128)S(1)} %broadcast_multiply_fusion.1), kind=kLoop, calls=%fused_computation.123 | loop fusion | flops 1568768 | bytes 2129920 | tf_op jit(solution)/shard_map/reduce_sum | solution.py:35
  81.1 2.1 %add_convert_fusion = bf16[32,128,128]{2,1,0:T(8,128)(2,1)} fusion(f32[32,128,128]{2,1,0:T(8,128)S(1)} %copy-done.1, f32[128]{0:T(128)S(1)} %copy-done.8, f32[128]{0:T(128)S(1)} %copy-done.9, f32[32,128]{1,0:T(8,128)S(1)} %add_rsqrt_fusion.1, f32[32,128]{1,0:T(8,128)S(1)} %broadcast_multiply_fusion.1), kind=kLoop, calls=%fused_computation.122 | loop fusion | flops 2621440 | bytes 3179520 | tf_op jit(solution)/shard_map/convert_element_type | solution.py:82
  83.2 21.1 %fusion.104 = (f32[4096]{0:T(1024)S(1)}, f32[4096,128]{1,0:T(8,128)S(1)}) fusion(f32[128]{0:T(128)S(1)} %copy-done.15, bf16[512,128]{1,0:T(8,128)(2,1)S(1)} %copy-done, bf16[4096,128]{1,0:T(8,128)(2,1)} %bitcast.155, bf16[128,512]{1,0:T(8,128)(2,1)S(1)} %copy-done.13, f32[512]{0:T(512)S(1)} %copy-done.14, f32[128]{0:T(128)S(1)} %copy-done.16, ...), kind=kOutput, calls=%fused_computation.249 | convolution fusion | flops 1214771200 | bytes 4475904 | tf_op jit(solution)/shard_map/dot_general | solution.py:88
  104.4 1.3 multiply_reduce_fusion
  105.7 1.9 %multiply_convert_fusion = bf16[4096,128]{1,0:T(8,128)(2,1)S(1)} fusion(f32[4096,128]{1,0:T(8,128)S(1)} %get-tuple-element.140, f32[128]{0:T(128)S(1)} %copy-done.10, f32[128]{0:T(128)S(1)} %copy-done.11, f32[4096]{0:T(1024)S(1)} %add_rsqrt_fusion, f32[4096]{0:T(1024)S(1)} %broadcast_multiply_fusion, f32[4096]{0:T(1024)S(1)} %convert_bitcast_fusion), kind=kLoop, calls=%fused_computation.120 | loop fusion | flops 3145728 | bytes 3195904 | tf_op jit(solution)/shard_map/convert_element_type | solution.py:92
  107.7 1.9 %collective-permute-start.7 = (bf16[1,128,128]{2,1,0:T(8,128)(2,1)S(1)}, bf16[1,128,128]{2,1,0:T(8,128)(2,1)S(1)}, u32[]{:S(2)}, u32[]{:S(2)}) collective-permute-start(bf16[1,128,128]{2,1,0:T(8,128)(2,1)S(1)} %get-tuple-element.86), channel_id=1, source_target_pairs={{0,8},{8,16},{16,24},{24,0},{1,9},{9,17},{17,25},{25,1},{2,10},{10... | collective-permute-start | bytes 98312 | tf_op jit(solution)/shard_map/ppermute | solution.py:24
  109.6 1.1 collective-permute-start.8
  110.7 1.9 %collective-permute-done.7 = bf16[1,128,128]{2,1,0:T(8,128)(2,1)S(1)} collective-permute-done((bf16[1,128,128]{2,1,0:T(8,128)(2,1)S(1)}, bf16[1,128,128]{2,1,0:T(8,128)(2,1)S(1)}, u32[]{:S(2)}, u32[]{:S(2)}) %collective-permute-start.7) | collective-permute-done | bytes 32800 | tf_op jit(solution)/shard_map/ppermute | solution.py:24
  112.6 1.0 collective-permute-done.8
  113.6 2.3 %collective-permute-start.10 = (bf16[34,1,128]{2,1,0:T(2,128)(2,1)S(1)}, bf16[34,1,128]{2,1,0:T(2,128)(2,1)S(1)}, u32[]{:S(2)}, u32[]{:S(2)}) collective-permute-start(bf16[34,1,128]{2,1,0:T(2,128)(2,1)S(1)} %get-tuple-element.77), channel_id=1, source_target_pairs={{1,0},{2,1},{3,2},{4,3},{5,4},{6,5},{7,6},{0,7},{9,8},{10,9},{11,1... | collective-permute-start | bytes 26120 | tf_op jit(solution)/shard_map/ppermute | solution.py:26
  115.9 1.4 %collective-permute-done.10 = bf16[34,1,128]{2,1,0:T(2,128)(2,1)S(1)} collective-permute-done((bf16[34,1,128]{2,1,0:T(2,128)(2,1)S(1)}, bf16[34,1,128]{2,1,0:T(2,128)(2,1)S(1)}, u32[]{:S(2)}, u32[]{:S(2)}) %collective-permute-start.10) | collective-permute-done | bytes 8736 | tf_op jit(solution)/shard_map/ppermute | solution.py:26
  117.3 3.5 %collective-permute-done.9 = bf16[34,1,128]{2,1,0:T(2,128)(2,1)S(1)} collective-permute-done((bf16[34,1,128]{2,1,0:T(2,128)(2,1)S(1)}, bf16[34,1,128]{2,1,0:T(2,128)(2,1)S(1)}, u32[]{:S(2)}, u32[]{:S(2)}) %collective-permute-start.9) | collective-permute-done | bytes 8736 | tf_op jit(solution)/shard_map/ppermute | solution.py:24
  120.9 0.5 pad_maximum_fusion.1
  121.6 1.2 collective-permute-done.11
  122.8 3.9 %collective-permute-done.12 = bf16[1,130,128]{2,1,0:T(8,128)(2,1)S(1)} collective-permute-done((bf16[1,130,128]{2,1,0:T(8,128)(2,1)S(1)}, bf16[1,130,128]{2,1,0:T(8,128)(2,1)S(1)}, u32[]{:S(2)}, u32[]{:S(2)}) %collective-permute-start.12) | collective-permute-done | bytes 33312 | tf_op jit(solution)/shard_map/ppermute | solution.py:14
  126.7 0.8 fusion.102
  127.5 4.1 %collective-permute-done.13 = bf16[1,130,128]{2,1,0:T(8,128)(2,1)S(1)} collective-permute-done((bf16[1,130,128]{2,1,0:T(8,128)(2,1)S(1)}, bf16[1,130,128]{2,1,0:T(8,128)(2,1)S(1)}, u32[]{:S(2)}, u32[]{:S(2)}) %collective-permute-start.13) | collective-permute-done | bytes 33312 | tf_op jit(solution)/shard_map/ppermute | solution.py:14
  131.7 0.4 reshape.177
  132.2 0.8 fusion.99
  133.0 0.3 convolution_add_fusion.8
  133.3 0.3 convolution_add_fusion.7
  133.6 0.3 convolution_add_fusion.6
  133.9 0.3 convolution_add_fusion.5
  134.2 0.3 convolution_add_fusion.4
  134.5 0.3 convolution_add_fusion.3
  134.8 0.3 convolution_add_fusion.2
  135.1 1.1 fusion.61
  (57 shorter events, 0.6 us)
Async XLA Ops:
  0.0 83.2 %copy-start = (bf16[512,128]{1,0:T(8,128)(2,1)S(1)}, bf16[512,128]{1,0:T(8,128)(2,1)}, u32[]{:S(2)}) copy-start(bf16[512,128]{1,0:T(8,128)(2,1)} %param.31) | copy-start | bytes 393220
  0.0 13.8 %copy-start.6 = (s32[32,128]{1,0:T(8,128)S(1)}, s32[32,128]{1,0:T(8,128)}, u32[]{:S(2)}) copy-start(s32[32,128]{1,0:T(8,128)} %param.24) | copy-start | bytes 49156
  1.0 7.4 %collective-permute-start = (bf16[3,128,128]{2,1,0:T(8,128)(2,1)S(1)}, bf16[3,128,128]{2,1,0:T(8,128)(2,1)S(1)}, u32[]{:S(2)}, u32[]{:S(2)}) collective-permute-start(bf16[3,128,128]{2,1,0:T(8,128)(2,1)S(1)} %get-tuple-element.89), channel_id=1, source_target_pairs={{0,8},{8,16},{16,24},{24,0},{1,9},{9,17},{17,25},{25,1},{2,10},{10... | collective-permute-start | bytes 294920 | tf_op jit(solution)/shard_map/ppermute | solution.py:24
  4.0 6.1 %collective-permute-start.1 = (bf16[3,128,128]{2,1,0:T(8,128)(2,1)S(1)}, bf16[3,128,128]{2,1,0:T(8,128)(2,1)S(1)}, u32[]{:S(2)}, u32[]{:S(2)}) collective-permute-start(bf16[3,128,128]{2,1,0:T(8,128)(2,1)S(1)} %get-tuple-element.88), channel_id=1, source_target_pairs={{8,0},{16,8},{24,16},{0,24},{9,1},{17,9},{25,17},{1,25},{10,2},{18... | collective-permute-start | bytes 294920 | tf_op jit(solution)/shard_map/ppermute | solution.py:26
  10.2 5.3 %collective-permute-start.2 = (bf16[38,3,128]{2,1,0:T(4,128)(2,1)S(1)}, bf16[38,3,128]{2,1,0:T(4,128)(2,1)S(1)}, u32[]{:S(2)}, u32[]{:S(2)}) collective-permute-start(bf16[38,3,128]{2,1,0:T(4,128)(2,1)S(1)} %get-tuple-element.72), channel_id=1, source_target_pairs={{0,1},{1,2},{2,3},{3,4},{4,5},{5,6},{6,7},{7,0},{8,9},{9,10},{10,1... | collective-permute-start | bytes 87560 | tf_op jit(solution)/shard_map/ppermute | solution.py:24
  10.2 5.2 %collective-permute-start.3 = (bf16[38,3,128]{2,1,0:T(4,128)(2,1)S(1)}, bf16[38,3,128]{2,1,0:T(4,128)(2,1)S(1)}, u32[]{:S(2)}, u32[]{:S(2)}) collective-permute-start(bf16[38,3,128]{2,1,0:T(4,128)(2,1)S(1)} %get-tuple-element.73), channel_id=1, source_target_pairs={{1,0},{2,1},{3,2},{4,3},{5,4},{6,5},{7,6},{0,7},{9,8},{10,9},{11,1... | collective-permute-start | bytes 87560 | tf_op jit(solution)/shard_map/ppermute | solution.py:26
  16.0 2.9 %copy-start.5 = (f32[7,7,128]{2,1,0:T(8,128)S(1)}, f32[7,7,128]{2,1,0:T(8,128)}, u32[]{:S(2)}) copy-start(f32[7,7,128]{2,1,0:T(8,128)} %param.25) | copy-start | bytes 75268
  18.7 1.3 collective-permute-start.4
  20.1 5.1 %collective-permute-start.5 = (bf16[3,134,128]{2,1,0:T(8,128)(2,1)S(1)}, bf16[3,134,128]{2,1,0:T(8,128)(2,1)S(1)}, u32[]{:S(2)}, u32[]{:S(2)}) collective-permute-start(bf16[3,134,128]{2,1,0:T(8,128)(2,1)S(1)} %collective-permute-done.4), channel_id=1, source_target_pairs={{0,2},{2,0},{1,3},{3,1},{4,6},{6,4},{5,7},{7,5},{8,10},{10,8},{9,1... | collective-permute-start | bytes 308744 | tf_op jit(solution)/shard_map/ppermute | solution.py:14
  25.1 7.5 %collective-permute-start.6 = (bf16[3,134,128]{2,1,0:T(8,128)(2,1)S(1)}, bf16[3,134,128]{2,1,0:T(8,128)(2,1)S(1)}, u32[]{:S(2)}, u32[]{:S(2)}) collective-permute-start(bf16[3,134,128]{2,1,0:T(8,128)(2,1)S(1)} %collective-permute-done.5), channel_id=1, source_target_pairs={{0,4},{4,0},{1,5},{5,1},{2,6},{6,2},{3,7},{7,3},{8,12},{12,8},{9,1... | collective-permute-start | bytes 308744 | tf_op jit(solution)/shard_map/ppermute | solution.py:14
  33.7 11.2 %copy-start.12 = (f32[128]{0:T(128)S(1)}, f32[128]{0:T(128)}, u32[]{:S(2)}) copy-start(f32[128]{0:T(128)} %param.26) | copy-start | bytes 1540
  78.3 2.8 %copy-start.1 = (f32[32,128,128]{2,1,0:T(8,128)S(1)}, f32[32,128,128]{2,1,0:T(8,128)}, u32[]{:S(2)}) copy-start(f32[32,128,128]{2,1,0:T(8,128)} %get-tuple-element.54) | copy-start | bytes 6291460
  78.3 2.8 %copy-start.8 = (f32[128]{0:T(128)S(1)}, f32[128]{0:T(128)}, u32[]{:S(2)}) copy-start(f32[128]{0:T(128)} %param.28) | copy-start | bytes 1540
  78.3 2.8 %copy-start.9 = (f32[128]{0:T(128)S(1)}, f32[128]{0:T(128)}, u32[]{:S(2)}) copy-start(f32[128]{0:T(128)} %param.27) | copy-start | bytes 1540
  81.0 2.2 %copy-start.2 = (bf16[32,128,128]{2,1,0:T(8,128)(2,1)S(1)}, bf16[32,128,128]{2,1,0:T(8,128)(2,1)}, u32[]{:S(2)}) copy-start(bf16[32,128,128]{2,1,0:T(8,128)(2,1)} %param.23) | copy-start | bytes 3145732
  81.0 2.2 %copy-start.13 = (bf16[128,512]{1,0:T(8,128)(2,1)S(1)}, bf16[128,512]{1,0:T(8,128)(2,1)}, u32[]{:S(2)}) copy-start(bf16[128,512]{1,0:T(8,128)(2,1)} %param.29) | copy-start | bytes 393220
  81.1 2.2 %copy-start.14 = (f32[512]{0:T(512)S(1)}, f32[512]{0:T(512)}, u32[]{:S(2)}) copy-start(f32[512]{0:T(512)} %param.30) | copy-start | bytes 6148
  81.1 2.2 %copy-start.15 = (f32[128]{0:T(128)S(1)}, f32[128]{0:T(128)}, u32[]{:S(2)}) copy-start(f32[128]{0:T(128)} %param.32) | copy-start | bytes 1540
  81.1 2.2 %copy-start.16 = (f32[128]{0:T(128)S(1)}, f32[128]{0:T(128)}, u32[]{:S(2)}) copy-start(f32[128]{0:T(128)} %param.33) | copy-start | bytes 1540
  104.4 1.3 copy-start.10
  104.4 1.3 copy-start.11
  107.7 4.9 %collective-permute-start.7 = (bf16[1,128,128]{2,1,0:T(8,128)(2,1)S(1)}, bf16[1,128,128]{2,1,0:T(8,128)(2,1)S(1)}, u32[]{:S(2)}, u32[]{:S(2)}) collective-permute-start(bf16[1,128,128]{2,1,0:T(8,128)(2,1)S(1)} %get-tuple-element.86), channel_id=1, source_target_pairs={{0,8},{8,16},{16,24},{24,0},{1,9},{9,17},{17,25},{25,1},{2,10},{10... | collective-permute-start | bytes 98312 | tf_op jit(solution)/shard_map/ppermute | solution.py:24
  109.6 4.0 %collective-permute-start.8 = (bf16[1,128,128]{2,1,0:T(8,128)(2,1)S(1)}, bf16[1,128,128]{2,1,0:T(8,128)(2,1)S(1)}, u32[]{:S(2)}, u32[]{:S(2)}) collective-permute-start(bf16[1,128,128]{2,1,0:T(8,128)(2,1)S(1)} %get-tuple-element.87), channel_id=1, source_target_pairs={{8,0},{16,8},{24,16},{0,24},{9,1},{17,9},{25,17},{1,25},{10,2},{18... | collective-permute-start | bytes 98312 | tf_op jit(solution)/shard_map/ppermute | solution.py:26
  113.6 3.7 %collective-permute-start.10 = (bf16[34,1,128]{2,1,0:T(2,128)(2,1)S(1)}, bf16[34,1,128]{2,1,0:T(2,128)(2,1)S(1)}, u32[]{:S(2)}, u32[]{:S(2)}) collective-permute-start(bf16[34,1,128]{2,1,0:T(2,128)(2,1)S(1)} %get-tuple-element.77), channel_id=1, source_target_pairs={{1,0},{2,1},{3,2},{4,3},{5,4},{6,5},{7,6},{0,7},{9,8},{10,9},{11,1... | collective-permute-start | bytes 26120 | tf_op jit(solution)/shard_map/ppermute | solution.py:26
  115.9 10.8 %copy-start.3 = (bf16[4,4,128,256]{3,2,1,0:T(8,128)(2,1)S(1)}, bf16[4,4,128,256]{3,2,1,0:T(8,128)(2,1)}, u32[]{:S(2)}) copy-start(bf16[4,4,128,256]{3,2,1,0:T(8,128)(2,1)} %param.36) | copy-start | bytes 3145732
  115.9 5.0 %collective-permute-start.9 = (bf16[34,1,128]{2,1,0:T(2,128)(2,1)S(1)}, bf16[34,1,128]{2,1,0:T(2,128)(2,1)S(1)}, u32[]{:S(2)}, u32[]{:S(2)}) collective-permute-start(bf16[34,1,128]{2,1,0:T(2,128)(2,1)S(1)} %get-tuple-element.76), channel_id=1, source_target_pairs={{0,1},{1,2},{2,3},{3,4},{4,5},{5,6},{6,7},{7,0},{8,9},{9,10},{10,1... | collective-permute-start | bytes 26120 | tf_op jit(solution)/shard_map/ppermute | solution.py:24
  121.5 1.3 collective-permute-start.11
  122.8 3.9 %collective-permute-start.12 = (bf16[1,130,128]{2,1,0:T(8,128)(2,1)S(1)}, bf16[1,130,128]{2,1,0:T(8,128)(2,1)S(1)}, u32[]{:S(2)}, u32[]{:S(2)}) collective-permute-start(bf16[1,130,128]{2,1,0:T(8,128)(2,1)S(1)} %collective-permute-done.11), channel_id=1, source_target_pairs={{0,2},{2,0},{1,3},{3,1},{4,6},{6,4},{5,7},{7,5},{8,10},{10,8},{9,1... | collective-permute-start | bytes 99848 | tf_op jit(solution)/shard_map/ppermute | solution.py:14
  126.7 4.8 %collective-permute-start.13 = (bf16[1,130,128]{2,1,0:T(8,128)(2,1)S(1)}, bf16[1,130,128]{2,1,0:T(8,128)(2,1)S(1)}, u32[]{:S(2)}, u32[]{:S(2)}) collective-permute-start(bf16[1,130,128]{2,1,0:T(8,128)(2,1)S(1)} %collective-permute-done.12), channel_id=1, source_target_pairs={{0,4},{4,0},{1,5},{5,1},{2,6},{6,2},{3,7},{7,3},{8,12},{12,8},{9,1... | collective-permute-start | bytes 99848 | tf_op jit(solution)/shard_map/ppermute | solution.py:14
  132.1 0.8 copy-start.7
  132.2 1.1 copy-start.4
where the time goes:
time: 136 us
  other arithmetic  56.1 us (41%)
  waiting for transfers between devices  32 us (24%)
  matrix products  24.3 us (18%)
  starting transfers between devices  17.1 us (13%)
  local copies, waits for them, and re-layouts  6.29 us (5%)
    reduce_sum x1, other arithmetic, layer_norm(): center = values - jnp.mean(values, axis=-1, keepdims=True)  33.4 us
    dot_general x1, matrix products, convnext_cells(): jnp.dot(hidden, project_weight, preferred_element_type=jnp.float32)  21.1 us
    ppermute x6, waiting for transfers between devices, swapped(): return lax.ppermute(block, axis, route)  18.8 us
    convert_element_type x1, other arithmetic, convnext_cells(): shifted = padded_in[:, col_tap:col_tap + breadth].astype(jnp.float32)  11.2 us
    ppermute x4, waiting for transfers between devices, extended_2(): lax.ppermute(tail, axis, [(i, (i + 1) % count) for i in range(count)])  10.5 us
    ppermute x4, starting transfers between devices, extended_2(): lax.ppermute(head, axis, [((i + 1) % count, i) for i in range(count)])  7.95 us
    ppermute x4, starting transfers between devices, extended_2(): lax.ppermute(tail, axis, [(i, (i + 1) % count) for i in range(count)])  4.93 us
    ppermute x6, starting transfers between devices, swapped(): return lax.ppermute(block, axis, route)  4.22 us
  transfers between devices with their start and end apart: 14, of which 13 were waited for; matrix products, arithmetic and copies ran while one was open for 2% of the time, Pallas kernels for 0%

commit v1 on v0

v1 whole, which is shorter than its diff:
```python
import functools

import jax
import jax.numpy as jnp
from jax import lax
from jax.experimental import pallas as pl
from jax.experimental.pallas import tpu as pltpu
from jax.sharding import PartitionSpec as P

MESH = pl.DeviceIdType.MESH
F32 = jnp.float32
BF16 = jnp.bfloat16
FAR = 8
EDGE = 16


def gelu(values):
    return 0.5 * values * (1.0 + lax.erf(values * 0.7071067811865476))


def layer_norm(values, gain, shift):
    center = values - jnp.mean(values, axis=-1, keepdims=True)
    spread = jnp.mean(center * center, axis=-1, keepdims=True)
    return center * lax.rsqrt(spread + 1e-06) * gain + shift


def body(
    feat,
    mask,
    dw,
    dw_bias,
    gain1,
    shift1,
    w1,
    b1,
    w2,
    b2,
    scale,
    gain2,
    shift2,
    cw_hbm,
    cb,
    out,
    slab,
    rows,
    corners,
    wide,
    ghost_wide,
    ext,
    taps,
    conv_out,
    nrm,
    side_out,
    side_in,
    stage,
    cw,
    coarse,
    slab_send,
    slab_recv,
    rows_send,
    rows_recv,
    corner_send,
    corner_recv,
    side_send,
    side_recv,
    stage_send,
    stage_recv,
    cw_sem,
):
    height, breadth, ch = feat.shape
    ks = dw.shape[0]
    rim = ks // 2
    blocks = breadth // FAR
    n_off = FAR + 2 * rim
    units = height // 4
    lat, lon = lax.axis_index("lat"), lax.axis_index("lon")
    n_lat, n_lon = lax.axis_size("lat"), lax.axis_size("lon")
    top = lat == n_lat - 1
    east, west = lax.rem(lon + 1, n_lon), lax.rem(lon + n_lon - 1, n_lon)
    north_lat = jnp.where(top, lat, lat + 1)
    north_lon = jnp.where(top, n_lon - 1 - lon, lon)
    north = (north_lat, north_lon)
    north_slot = jnp.where(top, 1, 0)
    south = (jnp.maximum(lat - 1, 0), lon)

    load_cw = pltpu.make_async_copy(cw_hbm, cw, cw_sem)
    load_cw.start()

    barrier = pltpu.get_barrier_semaphore()
    for target in ((lat, east), (lat, west), north):
        pl.semaphore_signal(barrier, inc=1, device_id=target, device_id_type=MESH)

    @pl.when(lat > 0)
    def _():
        pl.semaphore_signal(barrier, inc=1, device_id=south, device_id_type=MESH)

    pl.semaphore_wait(barrier, jnp.where(lat > 0, 4, 3))

    def remote(src, dst, send_sem, recv_sem, target):
        return pltpu.make_async_remote_copy(
            src_ref=src,
            dst_ref=dst,
            send_sem=send_sem,
            recv_sem=recv_sem,
            device_id=target,
            device_id_type=MESH,
        )

    to_east = remote(
        feat.at[:, breadth - EDGE : breadth], slab.at[0], slab_send.at[0], slab_recv.at[0], (lat, east)
    )
    to_west = remote(feat.at[:, 0:EDGE], slab.at[1], slab_send.at[1], slab_recv.at[1], (lat, west))
    to_east.start()
    to_west.start()
    rows_north = remote(
        feat.at[height - rim : height],
        rows.at[north_slot],
        rows_send.at[0],
        rows_recv.at[north_slot],
        north,
    )
    rows_south = remote(feat.at[0:rim], rows.at[1], rows_send.at[1], rows_recv.at[1], south)
    rows_north.start()

    @pl.when(lat > 0)
    def _():
        rows_south.start()

    row_id = lax.broadcasted_iota(jnp.int32, (ch, ch), 0)
    col_id = lax.broadcasted_iota(jnp.int32, (ch, ch), 1)
    diagonal = row_id == col_id
    nothing = jnp.zeros((ch, ch), BF16)
    for b in range(ks):
        for a in range(ks):
            block = jnp.where(diagonal, dw[a, b : b + 1, :], 0.0).astype(BF16)
            for o in range(2):
                i = (a + o) % 2
                d = (a + o - i) // 2
                base = ((d * ks + b) * 2 + i) * ch
                taps[base : base + ch, o * ch : (o + 1) * ch] = block
        base = ((0 * ks + b) * 2 + 0) * ch
        taps[base : base + ch, ch : 2 * ch] = nothing
        base = ((3 * ks + b) * 2 + 1) * ch
        taps[base : base + ch, 0:ch] = nothing

    def widen(r, carry):
        wide[r, FAR : FAR + breadth, :] = feat[r].astype(F32)
        return carry

    lax.fori_loop(0, height, widen, 0)

    to_east.wait_recv()
    to_west.wait_recv()

    corner_north = remote(
        slab.at[:, height - rim : height],
        corners.at[north_slot],
        corner_send.at[0],
        corner_recv.at[north_slot],
        north,
    )
    corner_south = remote(slab.at[:, 0:rim], corners.at[1], corner_send.at[1], corner_recv.at[1], south)
    corner_north.start()

    @pl.when(lat > 0)
    def _():
        corner_south.start()

    first = FAR - rim

    def spread_row(r, carry):
        wide[r, 0:FAR, :] = slab[0, r, EDGE - FAR : EDGE, :].astype(F32)
        wide[r, FAR + breadth :, :] = slab[1, r, 0:FAR, :].astype(F32)
        for o in range(n_off):
            ext[rim + r, o] = wide[r, pl.ds(first + o, blocks, stride=FAR), :].astype(BF16)
        return carry

    lax.fori_loop(0, height, spread_row, 0)

    turn = (
        lax.broadcasted_iota(jnp.int32, (blocks, blocks), 0)
        + lax.broadcasted_iota(jnp.int32, (blocks, blocks), 1)
        == blocks - 1
    ).astype(F32).astype(BF16)

    def ghost_tiles(slot, t):
        ghost_wide[t, FAR : FAR + breadth, :] = rows[slot, t].astype(F32)
        ghost_wide[t, 0:FAR, :] = corners[slot, 0, t, EDGE - FAR : EDGE, :].astype(F32)
        ghost_wide[t, FAR + breadth :, :] = corners[slot, 1, t, 0:FAR, :].astype(F32)
        return [
            ghost_wide[t, pl.ds(first + o, blocks, stride=FAR), :].astype(BF16) for o in range(n_off)
        ]

    def turned(tiles):
        flat = jnp.concatenate(tiles, axis=1)
        flat = jnp.dot(turn, flat, preferred_element_type=F32).astype(BF16)
        return [flat[:, o * ch : (o + 1) * ch] for o in range(len(tiles))][::-1]

    def ghost_rows():
        rows_north_in = remote(
            feat.at[0:rim], rows.at[1], rows_send.at[0], rows_recv.at[1], north
        )
        rows_north_in.wait_recv()
        remote(slab.at[:, 0:rim], corners.at[1], corner_send.at[0], corner_recv.at[1], north).wait_recv()

        @pl.when(top)
        def _():
            for t in range(rim):
                tiles = turned(ghost_tiles(1, rim - 1 - t))
                for o in range(n_off):
                    ext[rim + height + t, o] = tiles[o]

        @pl.when(jnp.logical_not(top))
        def _():
            for t in range(rim):
                tiles = ghost_tiles(1, t)
                for o in range(n_off):
                    ext[rim + height + t, o] = tiles[o]

        @pl.when(lat > 0)
        def _():
            remote(feat.at[0:rim], rows.at[0], rows_send.at[0], rows_recv.at[0], south).wait_recv()
            remote(
                slab.at[:, 0:rim], corners.at[0], corner_send.at[0], corner_recv.at[0], south
            ).wait_recv()
            for t in range(rim):
                tiles = ghost_tiles(0, t)
                for o in range(n_off):
                    ext[t, o] = tiles[o]

        @pl.when(lat == 0)
        def _():
            ext[0:rim] = jnp.zeros((rim, n_off, blocks, ch), BF16)

    def unit_at(step):
        inner = jnp.where(step < 2, step + 1, step - 1)
        return jnp.where(step == 2, 0, jnp.where(step == 3, units - 1, inner))

    def convolve(step):
        base = unit_at(step) * 4
        parts = []
        for pair in range(2):
            columns = []
            for d in range(4):
                for b in range(ks):
                    for i in range(2):
                        tile = ext[base + 2 * (pair + d) + i, b : b + FAR]
                        columns.append(tile.reshape(breadth, ch))
            parts.append(jnp.concatenate(columns, axis=1))
        lhs = jnp.concatenate(parts, axis=0)
        conv_out[lax.rem(step, 2)] = jnp.dot(lhs, taps[...], preferred_element_type=F32)

    order_row = lax.broadcasted_iota(jnp.int32, (breadth, breadth), 0)
    order_col = lax.broadcasted_iota(jnp.int32, (breadth, breadth), 1)
    placed = order_col == lax.rem(order_row, blocks) * FAR + order_row // blocks
    ones = jnp.ones((breadth, ch), BF16)

    def pointwise(step):
        base = unit_at(step) * 4
        for pair in range(2):
            part = conv_out[lax.rem(step, 2), pair * breadth : (pair + 1) * breadth, :]
            row = base + 2 * pair
            spatial = jnp.concatenate([part[:, 0:ch], part[:, ch : 2 * ch]], axis=0) + dw_bias[...]
            normed = layer_norm(spatial, gain1[...], shift1[...]).astype(BF16)
            hidden = []
            half = w1.shape[1] // 2
            for h in range(2):
                cut = slice(h * half, (h + 1) * half)
                lifted = jnp.dot(normed, w1[:, cut], preferred_element_type=F32) + b1[:, cut]
                hidden.append(gelu(lifted).astype(BF16))
            branch = jnp.dot(jnp.concatenate(hidden, axis=1), w2[...], preferred_element_type=F32)
            centre = jnp.concatenate(
                [ext[rim + row + i, rim : rim + FAR].reshape(breadth, ch) for i in range(2)], axis=0
            ).astype(F32)
            updated = centre + scale[...] * (branch + b2[...])
            picked = jnp.concatenate(
                [
                    jnp.where(placed, mask[pl.ds(row + i, 1), :].astype(F32), 0.0).astype(BF16)
                    for i in range(2)
                ],
                axis=0,
            )
            marks = jnp.dot(picked, ones, preferred_element_type=F32)
            normalized = marks * layer_norm(updated, gain2[...], shift2[...])
            for i in range(2):
                mine = normalized[i * breadth : (i + 1) * breadth]
                nrm[1 + row + i, 1 : 1 + FAR] = mine.astype(BF16).reshape(FAR, blocks, ch)
                at = lax.rem(step, 2) * 4 + 2 * pair + i
                side_out[0, step // 2, pl.ds(at, 1), :] = mine[breadth - 1 : breadth]
                side_out[1, step // 2, pl.ds(at, 1), :] = mine[0:1]

    def side_copy(way, pack):
        return remote(
            side_out.at[way, pack],
            side_in.at[way, pack],
            side_send.at[way, pack],
            side_recv.at[way, pack],
            (lat, east) if way == 0 else (lat, west),
        )

    def side_start(pack):
        for way in range(2):
            side_copy(way, pack).start()

    block_id = lax.broadcasted_iota(jnp.int32, (blocks, ch), 0)

    def side_finish(pack):
        for way in range(2):
            side_copy(way, pack).wait_recv()
        for part in range(2):
            base = unit_at(2 * pack + part) * 4
            for r in range(4):
                row = 1 + base + r
                at = part * 4 + r
                left = pltpu.roll(nrm[row, FAR].astype(F32), 1, 0)
                left = jnp.where(block_id == 0, side_in[0, pack, at : at + 1, :], left)
                nrm[row, 0] = left.astype(BF16)
                right = pltpu.roll(nrm[row, 1].astype(F32), blocks - 1, 0)
                right = jnp.where(block_id == blocks - 1, side_in[1, pack, at : at + 1, :], right)
                nrm[row, FAR + 1] = right.astype(BF16)

    stage_north = remote(
        nrm.at[height], stage.at[north_slot], stage_send.at[0], stage_recv.at[north_slot], north
    )
    stage_south = remote(nrm.at[1], stage.at[1], stage_send.at[1], stage_recv.at[1], south)

    def step_body(step, carry):
        @pl.when(step == 2)
        def _():
            ghost_rows()

        @pl.when(step == units - 2)
        def _():
            side_finish(1)
            stage_north.start()

            @pl.when(lat > 0)
            def _():
                stage_south.start()

        pointwise(step - 1)
        convolve(step)

        @pl.when(lax.rem(step, 2) == 0)
        def _():
            side_start(step // 2 - 1)

        return carry

    convolve(0)
    lax.fori_loop(1, units, step_body, 0)
    pointwise(units - 1)
    last = units // 2 - 1
    side_start(last)
    load_cw.wait()

    def shrink(first_row):
        parts = []
        for i in range(4):
            columns = []
            for a in range(4):
                for b in range(4):
                    tiles = [nrm[2 * (first_row + i) + a, 2 * o + b] for o in range(FAR // 2)]
                    columns.append(jnp.concatenate(tiles, axis=0))
            parts.append(jnp.concatenate(columns, axis=1))
        lhs = jnp.concatenate(parts, axis=0)
        total = jnp.dot(lhs, cw[...], preferred_element_type=F32) + cb[...]
        per_row = breadth // 2
        for i in range(4):
            for o in range(FAR // 2):
                at = i * per_row + o * blocks
                for h in range(total.shape[1] // 128):
                    lanes = slice(h * 128, (h + 1) * 128)
                    coarse[i, h, pl.ds(o, blocks, stride=FAR // 2), :] = total[at : at + blocks, lanes]
        for i in range(4):
            for h in range(total.shape[1] // 128):
                out[first_row + i, :, h * 128 : (h + 1) * 128] = coarse[i, h].astype(BF16)

    for pack in range(last):
        if pack != 1:
            side_finish(pack)

    remote(nrm.at[1], stage.at[1], stage_send.at[0], stage_recv.at[1], north).wait_recv()

    @pl.when(top)
    def _():
        tiles = turned([stage[1, o] for o in range(FAR + 2)])
        for o in range(FAR + 2):
            nrm[height + 1, o] = tiles[o]

    @pl.when(jnp.logical_not(top))
    def _():
        nrm[height + 1] = stage[1]

    @pl.when(lat > 0)
    def _():
        remote(nrm.at[1], stage.at[0], stage_send.at[0], stage_recv.at[0], south).wait_recv()
        nrm[0] = stage[0]

    @pl.when(lat == 0)
    def _():
        nrm[0] = jnp.zeros((FAR + 2, blocks, ch), BF16)

    groups = height // 8
    for g in range(groups):
        if g == groups - 2:
            side_finish(last)
        shrink(4 * g)

    to_east.wait_send()
    to_west.wait_send()
    rows_north.wait_send()
    corner_north.wait_send()
    stage_north.wait_send()
    for pack in range(units // 2):
        for way in range(2):
            side_copy(way, pack).wait_send()

    @pl.when(lat > 0)
    def _():
        rows_south.wait_send()
        corner_south.wait_send()
        stage_south.wait_send()


def local(
    features,
    land_mask,
    dw_weight,
    dw_bias,
    norm_gain,
    norm_shift,
    expand_weight,
    expand_bias,
    project_weight,
    project_bias,
    layer_scale,
    out_gain,
    out_shift,
    coarse_weight,
    coarse_bias,
):
    height, breadth, ch = features.shape
    ks = dw_weight.shape[0]
    rim = ks // 2
    blocks = breadth // FAR
    n_off = FAR + 2 * rim
    packs = height // 8
    outs = coarse_weight.shape[3]
    coarse_flat = coarse_weight.reshape(-1, outs)
    line = lambda v: v.reshape(1, -1)
    vmem = pl.BlockSpec(memory_space=pltpu.VMEM)
    dma = pltpu.SemaphoreType.DMA
    return pl.pallas_call(
        body,
        out_shape=jax.ShapeDtypeStruct((height // 2, breadth // 2, outs), BF16),
        in_specs=[vmem] * 13 + [pl.BlockSpec(memory_space=pl.ANY), vmem],
        out_specs=vmem,
        scratch_shapes=[
            pltpu.VMEM((2, height, EDGE, ch), BF16),
            pltpu.VMEM((2, rim, breadth, ch), BF16),
            pltpu.VMEM((2, 2, rim, EDGE, ch), BF16),
            pltpu.VMEM((height, breadth + 2 * FAR, ch), F32),
            pltpu.VMEM((rim, breadth + 2 * FAR, ch), F32),
            pltpu.VMEM((height + 2 * rim, n_off, blocks, ch), BF16),
            pltpu.VMEM((4 * ks * 2 * ch, 2 * ch), BF16),
            pltpu.VMEM((2, 2 * breadth, 2 * ch), F32),
            pltpu.VMEM((height + 2, FAR + 2, blocks, ch), BF16),
            pltpu.VMEM((2, packs, 8, ch), F32),
            pltpu.VMEM((2, packs, 8, ch), F32),
            pltpu.VMEM((2, FAR + 2, blocks, ch), BF16),
            pltpu.VMEM(coarse_flat.shape, BF16),
            pltpu.VMEM((4, outs // 128, breadth // 2, 128), F32),
            dma((2,)),
            dma((2,)),
            dma((2,)),
            dma((2,)),
            dma((2,)),
            dma((2,)),
            dma((2, packs)),
            dma((2, packs)),
            dma((2,)),
            dma((2,)),
            dma,
        ],
        compiler_params=pltpu.CompilerParams(
            collective_id=0, has_side_effects=True, vmem_limit_bytes=50 * 1024 * 1024
        ),
    )(
        features,
        land_mask,
        dw_weight,
        line(dw_bias),
        line(norm_gain),
        line(norm_shift),
        expand_weight,
        line(expand_bias),
        project_weight,
        line(project_bias),
        line(layer_scale),
        line(out_gain),
        line(out_shift),
        coarse_flat,
        line(coarse_bias),
    )


def solution(mesh):
    placed = (P("lat", "lon", None), P("lat", "lon")) + (P(),) * 13
    return jax.shard_map(
        local, mesh=mesh, in_specs=placed, out_specs=P("lat", "lon", None), check_vma=False
    )
```

time: 136 us -> 41.2 us (0.30)
  other arithmetic: 56.1 us -> 0 us
  waiting for transfers between devices: 32 us -> 0 us
  Pallas kernels: 0 us -> 29.2 us
  matrix products: 24.3 us -> 0 us
  starting transfers between devices: 17.1 us -> 0 us
  local copies, waits for them, and re-layouts: 6.29 us -> 11.1 us
    reduce_sum x3 -> x0, other arithmetic: 37.3 us -> none  [the longest x1 33.4 us: layer_norm(): center = values - jnp.mean(values, axis=-1, keepdims=True)]
    ppermute x14 -> x0, waiting for transfers between devices: 32 us -> none  [the longest x6 18.8 us: swapped(): return lax.ppermute(block, axis, route)]
    pallas_call x0 -> x1, Pallas kernels: none -> 29.2 us  [local(): pl.pallas_call(body, out_shape=jax.ShapeDtypeStruct((height // 2, breadth...]
    dot_general x9 -> x0, matrix products: 24.3 us -> none  [the longest x1 21.1 us: convnext_cells(): jnp.dot(hidden, project_weight, preferred_element_type=jnp.float32)]
    ppermute x14 -> x0, starting transfers between devices: 17.1 us -> none  [the longest x4 7.95 us: extended_2(): lax.ppermute(head, axis, [((i + 1) % count, i) for i in range(count)])]
    convert_element_type x4 -> x0, other arithmetic: 15.2 us -> none  [the longest x1 11.2 us: convnext_cells(): shifted = padded_in[:, col_tap:col_tap + breadth].astype(jnp.float32)]
    unnamed x38 -> x31, local copies, waits for them, and re-layouts: 2.68 us -> 11.1 us
    slice x5 -> x0, local copies, waits for them, and re-layouts: 2.59 us -> none  [the longest x1 1 us: extended_2(): head = lax.slice_in_dim(cells, 0, width, axis=dim)]
  transfers between devices with their start and end apart: 14 -> 0, of which waited for: 13 -> 0; matrix products, arithmetic and copies ran while one was open for 2% -> 0% of each run, Pallas kernels for 0% -> 0%
where the time goes in v1:
time: 41.2 us; the launch traced here: 40.4 us
  Pallas kernels  29.2 us (71%)
  local copies, waits for them, and re-layouts  11.1 us (27%)
    pallas_call x1, Pallas kernels, local(): pl.pallas_call(body, out_shape=jax.ShapeDtypeStruct((height // 2, breadth...  29.2 us
    unnamed x31, local copies, waits for them, and re-layouts  11.1 us

profile of v1, /device:TPU:0, one launch (start us, length us, event | category | flops | bytes accessed | tf_op | source)
XLA Modules:
  0.0 40.4 jit_solution(5219143399803921136)
XLA Ops:
  0.0 0.0 copy-start.5
  0.0 0.0 copy-start.6
  0.0 0.0 copy-start.8
  0.0 0.7 %copy-done.5 = s32[32,128]{1,0:T(8,128)S(1)} copy-done((s32[32,128]{1,0:T(8,128)S(1)}, s32[32,128]{1,0:T(8,128)}, u32[]{:S(2)}) %copy-start.5) | copy-done | bytes 16408
  0.7 0.0 copy-done.6
  0.7 0.0 copy-done.8
  0.7 0.0 copy-start
  0.7 1.2 %copy-done = bf16[32,128,128]{2,1,0:T(8,128)(2,1)S(1)} copy-done((bf16[32,128,128]{2,1,0:T(8,128)(2,1)S(1)}, bf16[32,128,128]{2,1,0:T(8,128)(2,1)}, u32[]{:S(2)}) %copy-start) | copy-done | bytes 1048600
  1.9 0.0 copy-start.1
  2.0 1.2 %copy-done.1 = bf16[4,4,128,256]{3,2,1,0:T(8,128)(2,1)S(1)} copy-done((bf16[4,4,128,256]{3,2,1,0:T(8,128)(2,1)S(1)}, bf16[4,4,128,256]{3,2,1,0:T(8,128)(2,1)}, u32[]{:S(2)}) %copy-start.1) | copy-done | bytes 1048600
  3.2 0.0 copy-start.2
  3.2 0.9 %copy-done.2 = bf16[128,512]{1,0:T(8,128)(2,1)S(1)} copy-done((bf16[128,512]{1,0:T(8,128)(2,1)S(1)}, bf16[128,512]{1,0:T(8,128)(2,1)}, u32[]{:S(2)}) %copy-start.2) | copy-done | bytes 131096
  4.1 0.0 copy-start.3
  4.1 0.9 %copy-done.3 = bf16[512,128]{1,0:T(8,128)(2,1)S(1)} copy-done((bf16[512,128]{1,0:T(8,128)(2,1)S(1)}, bf16[512,128]{1,0:T(8,128)(2,1)}, u32[]{:S(2)}) %copy-start.3) | copy-done | bytes 131096
  5.0 0.0 copy-start.4
  5.0 0.7 %copy-done.4 = f32[7,7,128]{2,1,0:T(8,128)S(1)} copy-done((f32[7,7,128]{2,1,0:T(8,128)S(1)}, f32[7,7,128]{2,1,0:T(8,128)}, u32[]{:S(2)}) %copy-start.4) | copy-done | bytes 25112
  5.7 0.0 copy-start.7
  5.7 0.7 %copy-done.7 = f32[256]{0:T(256)S(1)} copy-done((f32[256]{0:T(256)S(1)}, f32[256]{0:T(256)}, u32[]{:S(2)}) %copy-start.7) | copy-done | bytes 1048
  6.4 0.0 copy-start.9
  6.4 0.7 %copy-done.9 = f32[128]{0:T(128)S(1)} copy-done((f32[128]{0:T(128)S(1)}, f32[128]{0:T(128)}, u32[]{:S(2)}) %copy-start.9) | copy-done | bytes 536
  7.1 0.0 copy-start.10
  7.1 0.7 %copy-done.10 = f32[128]{0:T(128)S(1)} copy-done((f32[128]{0:T(128)S(1)}, f32[128]{0:T(128)}, u32[]{:S(2)}) %copy-start.10) | copy-done | bytes 536
  7.7 0.0 copy-start.11
  7.7 0.7 %copy-done.11 = f32[128]{0:T(128)S(1)} copy-done((f32[128]{0:T(128)S(1)}, f32[128]{0:T(128)}, u32[]{:S(2)}) %copy-start.11) | copy-done | bytes 536
  8.4 0.0 copy-start.12
  8.4 0.7 %copy-done.12 = f32[128]{0:T(128)S(1)} copy-done((f32[128]{0:T(128)S(1)}, f32[128]{0:T(128)}, u32[]{:S(2)}) %copy-start.12) | copy-done | bytes 536
  9.0 0.0 copy-start.13
  9.0 0.7 %copy-done.13 = f32[128]{0:T(128)S(1)} copy-done((f32[128]{0:T(128)S(1)}, f32[128]{0:T(128)}, u32[]{:S(2)}) %copy-start.13) | copy-done | bytes 536
  9.7 0.0 copy-start.14
  9.7 0.7 %copy-done.14 = f32[128]{0:T(128)S(1)} copy-done((f32[128]{0:T(128)S(1)}, f32[128]{0:T(128)}, u32[]{:S(2)}) %copy-start.14) | copy-done | bytes 536
  10.3 29.2 %shard_map.145 = bf16[16,64,256]{2,1,0:T(8,128)(2,1)S(1)} custom-call(bf16[32,128,128]{2,1,0:T(8,128)(2,1)S(1)} %copy-done, s32[32,128]{1,0:T(8,128)S(1)} %copy-done.5, f32[7,7,128]{2,1,0:T(8,128)S(1)} %copy-done.4, f32[1,128]{1,0:T(1,128)S(1)} %bitcast.13, f32[1,128]{1,0:T(1,128)S(1)} %bitcast.14, f32[1,128]{1,0:T(1,128)S(1)} %bitcast.15, ...), custom_call_target="tpu_custom_call" | custom-call | tf_op jit(solution)/shard_map/pallas_call | solution.py:454
  39.6 0.8 %copy.17 = bf16[16,64,256]{2,1,0:T(8,128)(2,1)} copy(bf16[16,64,256]{2,1,0:T(8,128)(2,1)S(1)} %shard_map.145) | data formatting | bytes 1048576
Async XLA Ops:
  0.0 0.7 %copy-start.5 = (s32[32,128]{1,0:T(8,128)S(1)}, s32[32,128]{1,0:T(8,128)}, u32[]{:S(2)}) copy-start(s32[32,128]{1,0:T(8,128)} %mask.1) | copy-start | bytes 49156
  0.0 0.7 %copy-start.6 = (f32[512]{0:T(512)S(1)}, f32[512]{0:T(512)}, u32[]{:S(2)}) copy-start(f32[512]{0:T(512)} %param.22) | copy-start | bytes 6148
  0.0 0.7 %copy-start.8 = (f32[128]{0:T(128)S(1)}, f32[128]{0:T(128)}, u32[]{:S(2)}) copy-start(f32[128]{0:T(128)} %param.18) | copy-start | bytes 1540
  0.7 1.2 %copy-start = (bf16[32,128,128]{2,1,0:T(8,128)(2,1)S(1)}, bf16[32,128,128]{2,1,0:T(8,128)(2,1)}, u32[]{:S(2)}) copy-start(bf16[32,128,128]{2,1,0:T(8,128)(2,1)} %feat.1) | copy-start | bytes 3145732
  1.9 1.2 %copy-start.1 = (bf16[4,4,128,256]{3,2,1,0:T(8,128)(2,1)S(1)}, bf16[4,4,128,256]{3,2,1,0:T(8,128)(2,1)}, u32[]{:S(2)}) copy-start(bf16[4,4,128,256]{3,2,1,0:T(8,128)(2,1)} %param.28) | copy-start | bytes 3145732
  3.2 0.9 %copy-start.2 = (bf16[128,512]{1,0:T(8,128)(2,1)S(1)}, bf16[128,512]{1,0:T(8,128)(2,1)}, u32[]{:S(2)}) copy-start(bf16[128,512]{1,0:T(8,128)(2,1)} %w1.1) | copy-start | bytes 393220
  4.1 0.9 %copy-start.3 = (bf16[512,128]{1,0:T(8,128)(2,1)S(1)}, bf16[512,128]{1,0:T(8,128)(2,1)}, u32[]{:S(2)}) copy-start(bf16[512,128]{1,0:T(8,128)(2,1)} %w2.1) | copy-start | bytes 393220
  5.0 0.7 %copy-start.4 = (f32[7,7,128]{2,1,0:T(8,128)S(1)}, f32[7,7,128]{2,1,0:T(8,128)}, u32[]{:S(2)}) copy-start(f32[7,7,128]{2,1,0:T(8,128)} %dw.1) | copy-start | bytes 75268
  5.7 0.7 %copy-start.7 = (f32[256]{0:T(256)S(1)}, f32[256]{0:T(256)}, u32[]{:S(2)}) copy-start(f32[256]{0:T(256)} %param.29) | copy-start | bytes 3076
  6.4 0.7 %copy-start.9 = (f32[128]{0:T(128)S(1)}, f32[128]{0:T(128)}, u32[]{:S(2)}) copy-start(f32[128]{0:T(128)} %param.19) | copy-start | bytes 1540
  7.1 0.7 %copy-start.10 = (f32[128]{0:T(128)S(1)}, f32[128]{0:T(128)}, u32[]{:S(2)}) copy-start(f32[128]{0:T(128)} %param.20) | copy-start | bytes 1540
  7.7 0.7 %copy-start.11 = (f32[128]{0:T(128)S(1)}, f32[128]{0:T(128)}, u32[]{:S(2)}) copy-start(f32[128]{0:T(128)} %param.24) | copy-start | bytes 1540
  8.4 0.7 %copy-start.12 = (f32[128]{0:T(128)S(1)}, f32[128]{0:T(128)}, u32[]{:S(2)}) copy-start(f32[128]{0:T(128)} %param.25) | copy-start | bytes 1540
  9.0 0.7 %copy-start.13 = (f32[128]{0:T(128)S(1)}, f32[128]{0:T(128)}, u32[]{:S(2)}) copy-start(f32[128]{0:T(128)} %param.26) | copy-start | bytes 1540
  9.7 0.7 %copy-start.14 = (f32[128]{0:T(128)S(1)}, f32[128]{0:T(128)}, u32[]{:S(2)}) copy-start(f32[128]{0:T(128)} %param.27) | copy-start | bytes 1540

commit v2 on v1

--- a/solution.py
+++ b/solution.py
@@ -1,5 +1,3 @@
-import functools
-
 import jax
 import jax.numpy as jnp
 from jax import lax
@@ -14,8 +12,24 @@
 EDGE = 16
 
 
-def gelu(values):
-    return 0.5 * values * (1.0 + lax.erf(values * 0.7071067811865476))
+ERF_FIT = (
+    0.7978842854499817,
+    0.03633416071534157,
+    -3.303515768493526e-05,
+    -5.5270647862926126e-05,
+    3.973660568590276e-06,
+    -1.337553072744413e-07,
+    1.813239114412113e-09,
+)
+ERF_END = 27.04
+
+
+def twice_gelu(values):
+    square = jnp.minimum(values * values, ERF_END)
+    slope = jnp.full_like(values, ERF_FIT[-1])
+    for coefficient in ERF_FIT[-2::-1]:
+        slope = slope * square + coefficient
+    return values + values * jnp.tanh(values * slope)
 
 
 def layer_norm(values, gain, shift):
@@ -24,49 +38,37 @@
     return center * lax.rsqrt(spread + 1e-06) * gain + shift
 
 
-def body(
-    feat,
-    mask,
-    dw,
-    dw_bias,
-    gain1,
-    shift1,
-    w1,
-    b1,
-    w2,
-    b2,
-    scale,
-    gain2,
-    shift2,
-    cw_hbm,
-    cb,
-    out,
-    slab,
-    rows,
-    corners,
-    wide,
-    ghost_wide,
-    ext,
-    taps,
-    conv_out,
-    nrm,
-    side_out,
-    side_in,
-    stage,
-    cw,
-    coarse,
-    slab_send,
-    slab_recv,
-    rows_send,
-    rows_recv,
-    corner_send,
-    corner_recv,
-    side_send,
-    side_recv,
-    stage_send,
-    stage_recv,
-    cw_sem,
-):
+def body(*refs):
+    sources, out, held = refs[:15], refs[15], refs[16:31]
+    (
+        slab,
+        rows,
+        corners,
+        wide,
+        ghost_wide,
+        ext,
+        taps,
+        conv_out,
+        nrm,
+        side_out,
+        side_in,
+        stage,
+        coarse,
+        slab_send,
+        slab_recv,
+        rows_send,
+        rows_recv,
+        corner_send,
+        corner_recv,
+        side_send,
+        side_recv,
+        stage_send,
+        stage_recv,
+        load_sem,
+    ) = refs[31:]
+    feat = sources[0]
+    near = held[0]
+    mask, dw, dw_bias, gain1, shift1, w1, b1, w2, b2, scale, gain2, shift2, cw, cb = held[1:]
     height, breadth, ch = feat.shape
     ks = dw.shape[0]
     rim = ks // 2
@@ -83,8 +85,10 @@
     north_slot = jnp.where(top, 1, 0)
     south = (jnp.maximum(lat - 1, 0), lon)
 
-    load_cw = pltpu.make_async_copy(cw_hbm, cw, cw_sem)
-    load_cw.start()
+    loads = [pltpu.make_async_copy(sources[k], held[k], load_sem.at[k]) for k in range(len(sources))]
+    first_loads = (0, 2)
+    for k in first_loads:
+        loads[k].start()
 
     barrier = pltpu.get_barrier_semaphore()
     for target in ((lat, east), (lat, west), north):
@@ -126,10 +130,15 @@
     def _():
         rows_south.start()
 
+    for k in range(len(sources)):
+        if k not in first_loads:
+            loads[k].start()
+
     row_id = lax.broadcasted_iota(jnp.int32, (ch, ch), 0)
     col_id = lax.broadcasted_iota(jnp.int32, (ch, ch), 1)
     diagonal = row_id == col_id
     nothing = jnp.zeros((ch, ch), BF16)
+    loads[2].wait()
     for b in range(ks):
         for a in range(ks):
             block = jnp.where(diagonal, dw[a, b : b + 1, :], 0.0).astype(BF16)
@@ -143,11 +152,21 @@
         base = ((3 * ks + b) * 2 + 1) * ch
         taps[base : base + ch, 0:ch] = nothing
 
-    def widen(r, carry):
-        wide[r, FAR : FAR + breadth, :] = feat[r].astype(F32)
+    first = FAR - rim
+
+    def pick(r, offsets):
+        for o in offsets:
+            ext[rim + r, o] = wide[r, pl.ds(first + o, blocks, stride=FAR), :].astype(BF16)
+
+    def widen(k, carry):
+        for r in range(4):
+            wide[4 * k + r, FAR : FAR + breadth, :] = near[4 * k + r].astype(F32)
+        for r in range(4):
+            pick(4 * k + r, range(rim, rim + FAR))
         return carry
 
-    lax.fori_loop(0, height, widen, 0)
+    loads[0].wait()
+    lax.fori_loop(0, height // 4, widen, 0)
 
     to_east.wait_recv()
     to_west.wait_recv()
@@ -166,16 +185,15 @@
     def _():
         corner_south.start()
 
-    first = FAR - rim
-
-    def spread_row(r, carry):
-        wide[r, 0:FAR, :] = slab[0, r, EDGE - FAR : EDGE, :].astype(F32)
-        wide[r, FAR + breadth :, :] = slab[1, r, 0:FAR, :].astype(F32)
-        for o in range(n_off):
-            ext[rim + r, o] = wide[r, pl.ds(first + o, blocks, stride=FAR), :].astype(BF16)
+    def widen_sides(k, carry):
+        for r in range(4):
+            wide[4 * k + r, 0:FAR, :] = slab[0, 4 * k + r, EDGE - FAR : EDGE, :].astype(F32)
+            wide[4 * k + r, FAR + breadth :, :] = slab[1, 4 * k + r, 0:FAR, :].astype(F32)
+        for r in range(4):
+            pick(4 * k + r, (*range(rim), *range(rim + FAR, n_off)))
         return carry
 
-    lax.fori_loop(0, height, spread_row, 0)
+    lax.fori_loop(0, height // 4, widen_sides, 0)
 
     turn = (
         lax.broadcasted_iota(jnp.int32, (blocks, blocks), 0)
@@ -267,12 +285,12 @@
             for h in range(2):
                 cut = slice(h * half, (h + 1) * half)
                 lifted = jnp.dot(normed, w1[:, cut], preferred_element_type=F32) + b1[:, cut]
-                hidden.append(gelu(lifted).astype(BF16))
+                hidden.append(twice_gelu(lifted).astype(BF16))
             branch = jnp.dot(jnp.concatenate(hidden, axis=1), w2[...], preferred_element_type=F32)
             centre = jnp.concatenate(
                 [ext[rim + row + i, rim : rim + FAR].reshape(breadth, ch) for i in range(2)], axis=0
             ).astype(F32)
-            updated = centre + scale[...] * (branch + b2[...])
+            updated = centre + scale[...] * (0.5 * branch + b2[...])
             picked = jnp.concatenate(
                 [
                     jnp.where(placed, mask[pl.ds(row + i, 1), :].astype(F32), 0.0).astype(BF16)
@@ -348,11 +366,15 @@
         return carry
 
     convolve(0)
+    for k in range(len(sources)):
+        if k not in first_loads and k < 13:
+            loads[k].wait()
     lax.fori_loop(1, units, step_body, 0)
     pointwise(units - 1)
     last = units // 2 - 1
     side_start(last)
-    load_cw.wait()
+    loads[13].wait()
+    loads[14].wait()
 
     def shrink(first_row):
         parts = []
@@ -449,44 +471,8 @@
     outs = coarse_weight.shape[3]
     coarse_flat = coarse_weight.reshape(-1, outs)
     line = lambda v: v.reshape(1, -1)
-    vmem = pl.BlockSpec(memory_space=pltpu.VMEM)
-    dma = pltpu.SemaphoreType.DMA
-    return pl.pallas_call(
-        body,
-        out_shape=jax.ShapeDtypeStruct((height // 2, breadth // 2, outs), BF16),
-        in_specs=[vmem] * 13 + [pl.BlockSpec(memory_space=pl.ANY), vmem],
-        out_specs=vmem,
-        scratch_shapes=[
-            pltpu.VMEM((2, height, EDGE, ch), BF16),
-            pltpu.VMEM((2, rim, breadth, ch), BF16),
-            pltpu.VMEM((2, 2, rim, EDGE, ch), BF16),
-            pltpu.VMEM((height, breadth + 2 * FAR, ch), F32),
-            pltpu.VMEM((rim, breadth + 2 * FAR, ch), F32),
-            pltpu.VMEM((height + 2 * rim, n_off, blocks, ch), BF16),
-            pltpu.VMEM((4 * ks * 2 * ch, 2 * ch), BF16),
-            pltpu.VMEM((2, 2 * breadth, 2 * ch), F32),
-            pltpu.VMEM((height + 2, FAR + 2, blocks, ch), BF16),
-            pltpu.VMEM((2, packs, 8, ch), F32),
-            pltpu.VMEM((2, packs, 8, ch), F32),
-            pltpu.VMEM((2, FAR + 2, blocks, ch), BF16),
-            pltpu.VMEM(coarse_flat.shape, BF16),
-            pltpu.VMEM((4, outs // 128, breadth // 2, 128), F32),
-            dma((2,)),
-            dma((2,)),
-            dma((2,)),
-            dma((2,)),
-            dma((2,)),
-            dma((2,)),
-            dma((2, packs)),
-            dma((2, packs)),
-            dma((2,)),
-            dma((2,)),
-            dma,
-        ],
-        compiler_params=pltpu.CompilerParams(
-            collective_id=0, has_side_effects=True, vmem_limit_bytes=50 * 1024 * 1024
-        ),
-    )(
+    anywhere = pl.BlockSpec(memory_space=pl.ANY)
+    arrays = (
         features,
         land_mask,
         dw_weight,
@@ -503,6 +489,43 @@
         coarse_flat,
         line(coarse_bias),
     )
+    dma = pltpu.SemaphoreType.DMA
+    return pl.pallas_call(
+        body,
+        out_shape=jax.ShapeDtypeStruct((height // 2, breadth // 2, outs), BF16),
+        in_specs=[anywhere] * len(arrays),
+        out_specs=pl.BlockSpec(memory_space=pltpu.VMEM),
+        scratch_shapes=[pltpu.VMEM(v.shape, v.dtype) for v in arrays]
+        + [
+            pltpu.VMEM((2, height, EDGE, ch), BF16),
+            pltpu.VMEM((2, rim, breadth, ch), BF16),
+            pltpu.VMEM((2, 2, rim, EDGE, ch), BF16),
+            pltpu.VMEM((height, breadth + 2 * FAR, ch), F32),
+            pltpu.VMEM((rim, breadth + 2 * FAR, ch), F32),
+            pltpu.VMEM((height + 2 * rim, n_off, blocks, ch), BF16),
+            pltpu.VMEM((4 * ks * 2 * ch, 2 * ch), BF16),
+            pltpu.VMEM((2, 2 * breadth, 2 * ch), F32),
+            pltpu.VMEM((height + 2, FAR + 2, blocks, ch), BF16),
+            pltpu.VMEM((2, packs, 8, ch), F32),
+            pltpu.VMEM((2, packs, 8, ch), F32),
+            pltpu.VMEM((2, FAR + 2, blocks, ch), BF16),
+            pltpu.VMEM((4, outs // 128, breadth // 2, 128), F32),
+            dma((2,)),
+            dma((2,)),
+            dma((2,)),
+            dma((2,)),
+            dma((2,)),
+            dma((2,)),
+            dma((2, packs)),
+            dma((2, packs)),
+            dma((2,)),
+            dma((2,)),
+            dma((len(arrays),)),
+        ],
+        compiler_params=pltpu.CompilerParams(
+            collective_id=0, has_side_effects=True, vmem_limit_bytes=56 * 1024 * 1024
+        ),
+    )(*arrays)
 
 
 def solution(mesh):

time: 41.2 us -> 35.1 us (0.85)
  local copies, waits for them, and re-layouts: 11.1 us -> 1.88 us
  Pallas kernels: 29.2 us -> 32.7 us
    unnamed x31 -> x1, local copies, waits for them, and re-layouts: 11.1 us -> 1.88 us
    pallas_call x1, Pallas kernels: 29.2 us -> 32.7 us  [local(): pl.pallas_call(body, out_shape=jax.ShapeDtypeStruct((height // 2, breadth...]
where the time goes in v2:
time: 35.1 us; the launch traced here: 34.5 us
  Pallas kernels  32.7 us (93%)
  local copies, waits for them, and re-layouts  1.88 us (5%)
    pallas_call x1, Pallas kernels, local(): pl.pallas_call(body, out_shape=jax.ShapeDtypeStruct((height // 2, breadth...  32.7 us
    unnamed x1, local copies, waits for them, and re-layouts  1.88 us

profile of v2, /device:TPU:0, one launch (start us, length us, event | category | flops | bytes accessed | tf_op | source)
XLA Modules:
  0.0 34.5 jit_solution(1986284849921266719)
XLA Ops:
  0.0 32.7 %shard_map.145 = bf16[16,64,256]{2,1,0:T(8,128)(2,1)} custom-call(bf16[32,128,128]{2,1,0:T(8,128)(2,1)} %refs_0_.1, s32[32,128]{1,0:T(8,128)} %refs_1_.1, f32[7,7,128]{2,1,0:T(8,128)} %refs_2_.1, f32[1,128]{1,0:T(1,128)} %bitcast.13, f32[1,128]{1,0:T(1,128)} %bitcast.14, f32[1,128]{1,0:T(1,128)} %bitcast.15, bf16[128,512]{1,0:T(8,128)(2,1)} %refs_6_.1, ...), custom_call_target="tpu_custom_call" | custom-call | tf_op jit(solution)/shard_map/pallas_call | solution.py:493
  32.7 1.9 %copy.17 = bf16[16,64,256]{2,1,0:T(8,128)(2,1)} copy(bf16[16,64,256]{2,1,0:T(8,128)(2,1)} %shard_map.145) | data formatting | bytes 1048576

commit v3 on v2

--- a/solution.py
+++ b/solution.py
@@ -1,3 +1,5 @@
+import functools
+
 import jax
 import jax.numpy as jnp
 from jax import lax
@@ -254,43 +256,46 @@
         inner = jnp.where(step < 2, step + 1, step - 1)
         return jnp.where(step == 2, 0, jnp.where(step == 3, units - 1, inner))
 
-    def convolve(step):
+    def convolve(step, d):
         base = unit_at(step) * 4
         parts = []
         for pair in range(2):
             columns = []
-            for d in range(4):
-                for b in range(ks):
-                    for i in range(2):
-                        tile = ext[base + 2 * (pair + d) + i, b : b + FAR]
-                        columns.append(tile.reshape(breadth, ch))
+            for b in range(ks):
+                for i in range(2):
+                    tile = ext[base + 2 * (pair + d) + i, b : b + FAR]
+                    columns.append(tile.reshape(breadth, ch))
             parts.append(jnp.concatenate(columns, axis=1))
         lhs = jnp.concatenate(parts, axis=0)
-        conv_out[lax.rem(step, 2)] = jnp.dot(lhs, taps[...], preferred_element_type=F32)
+        depth = 2 * ks * ch
+        slot = lax.rem(step, 2)
+        added = jnp.dot(lhs, taps[d * depth : (d + 1) * depth, :], preferred_element_type=F32)
+        conv_out[slot] = added if d == 0 else conv_out[slot] + added
 
     order_row = lax.broadcasted_iota(jnp.int32, (breadth, breadth), 0)
     order_col = lax.broadcasted_iota(jnp.int32, (breadth, breadth), 1)
     placed = order_col == lax.rem(order_row, blocks) * FAR + order_row // blocks
     ones = jnp.ones((breadth, ch), BF16)
 
-    def pointwise(step):
+    def pointwise(step, between):
         base = unit_at(step) * 4
-        for pair in range(2):
-            part = conv_out[lax.rem(step, 2), pair * breadth : (pair + 1) * breadth, :]
+        slot = lax.rem(step, 2)
+        half = w1.shape[1] // 2
+        cuts = [slice(h * half, (h + 1) * half) for h in range(2)]
+
+        def first_norm(pair):
+            part = conv_out[slot, pair * breadth : (pair + 1) * breadth, :]
+            spatial = jnp.concatenate([part[:, 0:ch], part[:, ch : 2 * ch]], axis=0) + dw_bias[...]
+            return layer_norm(spatial, gain1[...], shift1[...]).astype(BF16)
+
+        def lift(normed, cut):
+            return jnp.dot(normed, w1[:, cut], preferred_element_type=F32) + b1[:, cut]
+
+        def project(hidden):
+            return jnp.dot(jnp.concatenate(hidden, axis=1), w2[...], preferred_element_type=F32)
+
+        def spot(pair):
             row = base + 2 * pair
-            spatial = jnp.concatenate([part[:, 0:ch], part[:, ch : 2 * ch]], axis=0) + dw_bias[...]
-            normed = layer_norm(spatial, gain1[...], shift1[...]).astype(BF16)
-            hidden = []
-            half = w1.shape[1] // 2
-            for h in range(2):
-                cut = slice(h * half, (h + 1) * half)
-                lifted = jnp.dot(normed, w1[:, cut], preferred_element_type=F32) + b1[:, cut]
-                hidden.append(twice_gelu(lifted).astype(BF16))
-            branch = jnp.dot(jnp.concatenate(hidden, axis=1), w2[...], preferred_element_type=F32)
-            centre = jnp.concatenate(
-                [ext[rim + row + i, rim : rim + FAR].reshape(breadth, ch) for i in range(2)], axis=0
-            ).astype(F32)
-            updated = centre + scale[...] * (0.5 * branch + b2[...])
             picked = jnp.concatenate(
                 [
                     jnp.where(placed, mask[pl.ds(row + i, 1), :].astype(F32), 0.0).astype(BF16)
@@ -298,14 +303,37 @@
                 ],
                 axis=0,
             )
-            marks = jnp.dot(picked, ones, preferred_element_type=F32)
-            normalized = marks * layer_norm(updated, gain2[...], shift2[...])
+            return jnp.dot(picked, ones, preferred_element_type=F32)
+
+        def finish(pair, branch):
+            row = base + 2 * pair
+            centre = jnp.concatenate(
+                [ext[rim + row + i, rim : rim + FAR].reshape(breadth, ch) for i in range(2)], axis=0
+            ).astype(F32)
+            updated = centre + scale[...] * (0.5 * branch + b2[...])
+            normalized = spot(pair) * layer_norm(updated, gain2[...], shift2[...])
             for i in range(2):
                 mine = normalized[i * breadth : (i + 1) * breadth]
                 nrm[1 + row + i, 1 : 1 + FAR] = mine.astype(BF16).reshape(FAR, blocks, ch)
-                at = lax.rem(step, 2) * 4 + 2 * pair + i
+                at = slot * 4 + 2 * pair + i
                 side_out[0, step // 2, pl.ds(at, 1), :] = mine[breadth - 1 : breadth]
                 side_out[1, step // 2, pl.ds(at, 1), :] = mine[0:1]
+
+        normed = [first_norm(pair) for pair in range(2)]
+        work = [(pair, h) for pair in range(2) for h in range(2)]
+        hidden = [[], []]
+        lifted = lift(normed[0], cuts[0])
+        for k, (pair, h) in enumerate(work):
+            if k + 1 < len(work):
+                coming = lift(normed[work[k + 1][0]], cuts[work[k + 1][1]])
+            if between:
+                between[k]()
+            hidden[pair].append(twice_gelu(lifted).astype(BF16))
+            if k + 1 < len(work):
+                lifted = coming
+            if k == 2:
+                finish(0, project(hidden[0]))
+        finish(1, project(hidden[1]))
 
     def side_copy(way, pack):
         return remote(
@@ -356,8 +384,7 @@
             def _():
                 stage_south.start()
 
-        pointwise(step - 1)
-        convolve(step)
+        pointwise(step - 1, [functools.partial(convolve, step, d) for d in range(4)])
 
         @pl.when(lax.rem(step, 2) == 0)
         def _():
@@ -365,12 +392,13 @@
 
         return carry
 
-    convolve(0)
+    for d in range(4):
+        convolve(0, d)
     for k in range(len(sources)):
         if k not in first_loads and k < 13:
             loads[k].wait()
     lax.fori_loop(1, units, step_body, 0)
-    pointwise(units - 1)
+    pointwise(units - 1, [])
     last = units // 2 - 1
     side_start(last)
     loads[13].wait()
@@ -471,7 +499,7 @@
     outs = coarse_weight.shape[3]
     coarse_flat = coarse_weight.reshape(-1, outs)
     line = lambda v: v.reshape(1, -1)
-    anywhere = pl.BlockSpec(memory_space=pl.ANY)
+    anywhere = pl.BlockSpec(memory_space=pltpu.HBM)
     arrays = (
         features,
         land_mask,
@@ -523,7 +551,7 @@
             dma((len(arrays),)),
         ],
         compiler_params=pltpu.CompilerParams(
-            collective_id=0, has_side_effects=True, vmem_limit_bytes=56 * 1024 * 1024
+            collective_id=0, has_side_effects=True, vmem_limit_bytes=40 * 1024 * 1024
         ),
     )(*arrays)
 

time: 35.1 us -> 43.4 us (1.24)
  local copies, waits for them, and re-layouts: 1.88 us -> 11.1 us
  Pallas kernels: 32.7 us -> 31.5 us
    unnamed x1 -> x31, local copies, waits for them, and re-layouts: 1.88 us -> 11.1 us
    pallas_call x1, Pallas kernels: 32.7 us -> 31.5 us  [local(): pl.pallas_call(body, out_shape=jax.ShapeDtypeStruct((height // 2, breadth...]
where the time goes in v3:
time: 43.4 us; the launch traced here: 42.7 us
  Pallas kernels  31.5 us (73%)
  local copies, waits for them, and re-layouts  11.1 us (26%)
    pallas_call x1, Pallas kernels, local(): pl.pallas_call(body, out_shape=jax.ShapeDtypeStruct((height // 2, breadth...  31.5 us
    unnamed x31, local copies, waits for them, and re-layouts  11.1 us

profile of v3, /device:TPU:0, one launch (start us, length us, event | category | flops | bytes accessed | tf_op | source)
XLA Modules:
  0.0 42.7 jit_solution(2752173645214129797)
XLA Ops:
  0.0 0.0 copy-start.5
  0.0 0.0 copy-start.6
  0.0 0.0 copy-start.8
  0.0 0.7 %copy-done.5 = s32[32,128]{1,0:T(8,128)S(1)} copy-done((s32[32,128]{1,0:T(8,128)S(1)}, s32[32,128]{1,0:T(8,128)}, u32[]{:S(2)}) %copy-start.5) | copy-done | bytes 16408
  0.7 0.0 copy-done.6
  0.7 0.0 copy-done.8
  0.7 0.0 copy-start
  0.7 1.2 %copy-done = bf16[32,128,128]{2,1,0:T(8,128)(2,1)S(1)} copy-done((bf16[32,128,128]{2,1,0:T(8,128)(2,1)S(1)}, bf16[32,128,128]{2,1,0:T(8,128)(2,1)}, u32[]{:S(2)}) %copy-start) | copy-done | bytes 1048600
  1.9 0.0 copy-start.1
  2.0 1.2 %copy-done.1 = bf16[4,4,128,256]{3,2,1,0:T(8,128)(2,1)S(1)} copy-done((bf16[4,4,128,256]{3,2,1,0:T(8,128)(2,1)S(1)}, bf16[4,4,128,256]{3,2,1,0:T(8,128)(2,1)}, u32[]{:S(2)}) %copy-start.1) | copy-done | bytes 1048600
  3.2 0.0 copy-start.2
  3.2 0.9 %copy-done.2 = bf16[128,512]{1,0:T(8,128)(2,1)S(1)} copy-done((bf16[128,512]{1,0:T(8,128)(2,1)S(1)}, bf16[128,512]{1,0:T(8,128)(2,1)}, u32[]{:S(2)}) %copy-start.2) | copy-done | bytes 131096
  4.1 0.0 copy-start.3
  4.1 0.9 %copy-done.3 = bf16[512,128]{1,0:T(8,128)(2,1)S(1)} copy-done((bf16[512,128]{1,0:T(8,128)(2,1)S(1)}, bf16[512,128]{1,0:T(8,128)(2,1)}, u32[]{:S(2)}) %copy-start.3) | copy-done | bytes 131096
  5.0 0.0 copy-start.4
  5.0 0.7 %copy-done.4 = f32[7,7,128]{2,1,0:T(8,128)S(1)} copy-done((f32[7,7,128]{2,1,0:T(8,128)S(1)}, f32[7,7,128]{2,1,0:T(8,128)}, u32[]{:S(2)}) %copy-start.4) | copy-done | bytes 25112
  5.7 0.0 copy-start.7
  5.7 0.7 %copy-done.7 = f32[256]{0:T(256)S(1)} copy-done((f32[256]{0:T(256)S(1)}, f32[256]{0:T(256)}, u32[]{:S(2)}) %copy-start.7) | copy-done | bytes 1048
  6.4 0.0 copy-start.9
  6.4 0.7 %copy-done.9 = f32[128]{0:T(128)S(1)} copy-done((f32[128]{0:T(128)S(1)}, f32[128]{0:T(128)}, u32[]{:S(2)}) %copy-start.9) | copy-done | bytes 536
  7.1 0.0 copy-start.10
  7.1 0.7 %copy-done.10 = f32[128]{0:T(128)S(1)} copy-done((f32[128]{0:T(128)S(1)}, f32[128]{0:T(128)}, u32[]{:S(2)}) %copy-start.10) | copy-done | bytes 536
  7.7 0.0 copy-start.11
  7.7 0.7 %copy-done.11 = f32[128]{0:T(128)S(1)} copy-done((f32[128]{0:T(128)S(1)}, f32[128]{0:T(128)}, u32[]{:S(2)}) %copy-start.11) | copy-done | bytes 536
  8.4 0.0 copy-start.12
  8.4 0.7 %copy-done.12 = f32[128]{0:T(128)S(1)} copy-done((f32[128]{0:T(128)S(1)}, f32[128]{0:T(128)}, u32[]{:S(2)}) %copy-start.12) | copy-done | bytes 536
  9.0 0.0 copy-start.13
  9.0 0.7 %copy-done.13 = f32[128]{0:T(128)S(1)} copy-done((f32[128]{0:T(128)S(1)}, f32[128]{0:T(128)}, u32[]{:S(2)}) %copy-start.13) | copy-done | bytes 536
  9.7 0.0 copy-start.14
  9.7 0.7 %copy-done.14 = f32[128]{0:T(128)S(1)} copy-done((f32[128]{0:T(128)S(1)}, f32[128]{0:T(128)}, u32[]{:S(2)}) %copy-start.14) | copy-done | bytes 536
  10.3 31.5 %shard_map.145 = bf16[16,64,256]{2,1,0:T(8,128)(2,1)S(1)} custom-call(bf16[32,128,128]{2,1,0:T(8,128)(2,1)S(1)} %copy-done, s32[32,128]{1,0:T(8,128)S(1)} %copy-done.5, f32[7,7,128]{2,1,0:T(8,128)S(1)} %copy-done.4, f32[1,128]{1,0:T(1,128)S(1)} %bitcast.13, f32[1,128]{1,0:T(1,128)S(1)} %bitcast.14, f32[1,128]{1,0:T(1,128)S(1)} %bitcast.15, ...), custom_call_target="tpu_custom_call" | custom-call | tf_op jit(solution)/shard_map/pallas_call | solution.py:521
  41.9 0.8 %copy.17 = bf16[16,64,256]{2,1,0:T(8,128)(2,1)} copy(bf16[16,64,256]{2,1,0:T(8,128)(2,1)S(1)} %shard_map.145) | data formatting | bytes 1048576
Async XLA Ops:
  0.0 0.7 %copy-start.5 = (s32[32,128]{1,0:T(8,128)S(1)}, s32[32,128]{1,0:T(8,128)}, u32[]{:S(2)}) copy-start(s32[32,128]{1,0:T(8,128)} %refs_1_.1) | copy-start | bytes 49156
  0.0 0.7 %copy-start.6 = (f32[512]{0:T(512)S(1)}, f32[512]{0:T(512)}, u32[]{:S(2)}) copy-start(f32[512]{0:T(512)} %param.22) | copy-start | bytes 6148
  0.0 0.7 %copy-start.8 = (f32[128]{0:T(128)S(1)}, f32[128]{0:T(128)}, u32[]{:S(2)}) copy-start(f32[128]{0:T(128)} %param.18) | copy-start | bytes 1540
  0.7 1.2 %copy-start = (bf16[32,128,128]{2,1,0:T(8,128)(2,1)S(1)}, bf16[32,128,128]{2,1,0:T(8,128)(2,1)}, u32[]{:S(2)}) copy-start(bf16[32,128,128]{2,1,0:T(8,128)(2,1)} %refs_0_.1) | copy-start | bytes 3145732
  1.9 1.2 %copy-start.1 = (bf16[4,4,128,256]{3,2,1,0:T(8,128)(2,1)S(1)}, bf16[4,4,128,256]{3,2,1,0:T(8,128)(2,1)}, u32[]{:S(2)}) copy-start(bf16[4,4,128,256]{3,2,1,0:T(8,128)(2,1)} %param.28) | copy-start | bytes 3145732
  3.2 0.9 %copy-start.2 = (bf16[128,512]{1,0:T(8,128)(2,1)S(1)}, bf16[128,512]{1,0:T(8,128)(2,1)}, u32[]{:S(2)}) copy-start(bf16[128,512]{1,0:T(8,128)(2,1)} %refs_6_.1) | copy-start | bytes 393220
  4.1 0.9 %copy-start.3 = (bf16[512,128]{1,0:T(8,128)(2,1)S(1)}, bf16[512,128]{1,0:T(8,128)(2,1)}, u32[]{:S(2)}) copy-start(bf16[512,128]{1,0:T(8,128)(2,1)} %refs_8_.1) | copy-start | bytes 393220
  5.0 0.7 %copy-start.4 = (f32[7,7,128]{2,1,0:T(8,128)S(1)}, f32[7,7,128]{2,1,0:T(8,128)}, u32[]{:S(2)}) copy-start(f32[7,7,128]{2,1,0:T(8,128)} %refs_2_.1) | copy-start | bytes 75268
  5.7 0.7 %copy-start.7 = (f32[256]{0:T(256)S(1)}, f32[256]{0:T(256)}, u32[]{:S(2)}) copy-start(f32[256]{0:T(256)} %param.29) | copy-start | bytes 3076
  6.4 0.7 %copy-start.9 = (f32[128]{0:T(128)S(1)}, f32[128]{0:T(128)}, u32[]{:S(2)}) copy-start(f32[128]{0:T(128)} %param.19) | copy-start | bytes 1540
  7.1 0.7 %copy-start.10 = (f32[128]{0:T(128)S(1)}, f32[128]{0:T(128)}, u32[]{:S(2)}) copy-start(f32[128]{0:T(128)} %param.20) | copy-start | bytes 1540
  7.7 0.7 %copy-start.11 = (f32[128]{0:T(128)S(1)}, f32[128]{0:T(128)}, u32[]{:S(2)}) copy-start(f32[128]{0:T(128)} %param.24) | copy-start | bytes 1540
  8.4 0.7 %copy-start.12 = (f32[128]{0:T(128)S(1)}, f32[128]{0:T(128)}, u32[]{:S(2)}) copy-start(f32[128]{0:T(128)} %param.25) | copy-start | bytes 1540
  9.0 0.7 %copy-start.13 = (f32[128]{0:T(128)S(1)}, f32[128]{0:T(128)}, u32[]{:S(2)}) copy-start(f32[128]{0:T(128)} %param.26) | copy-start | bytes 1540
  9.7 0.7 %copy-start.14 = (f32[128]{0:T(128)S(1)}, f32[128]{0:T(128)}, u32[]{:S(2)}) copy-start(f32[128]{0:T(128)} %param.27) | copy-start | bytes 1540

commit v4 on v3

--- a/solution.py
+++ b/solution.py
@@ -256,19 +256,20 @@
         inner = jnp.where(step < 2, step + 1, step - 1)
         return jnp.where(step == 2, 0, jnp.where(step == 3, units - 1, inner))
 
-    def convolve(step, d):
-        base = unit_at(step) * 4
+    def convolve(pack, d):
         parts = []
-        for pair in range(2):
-            columns = []
-            for b in range(ks):
-                for i in range(2):
-                    tile = ext[base + 2 * (pair + d) + i, b : b + FAR]
-                    columns.append(tile.reshape(breadth, ch))
-            parts.append(jnp.concatenate(columns, axis=1))
+        for part in range(2):
+            base = unit_at(2 * pack + part) * 4
+            for pair in range(2):
+                columns = []
+                for b in range(ks):
+                    for i in range(2):
+                        tile = ext[base + 2 * (pair + d) + i, b : b + FAR]
+                        columns.append(tile.reshape(breadth, ch))
+                parts.append(jnp.concatenate(columns, axis=1))
         lhs = jnp.concatenate(parts, axis=0)
         depth = 2 * ks * ch
-        slot = lax.rem(step, 2)
+        slot = lax.rem(pack, 2)
         added = jnp.dot(lhs, taps[d * depth : (d + 1) * depth, :], preferred_element_type=F32)
         conv_out[slot] = added if d == 0 else conv_out[slot] + added
 
@@ -277,14 +278,15 @@
     placed = order_col == lax.rem(order_row, blocks) * FAR + order_row // blocks
     ones = jnp.ones((breadth, ch), BF16)
 
-    def pointwise(step, between):
-        base = unit_at(step) * 4
-        slot = lax.rem(step, 2)
+    def pointwise(pack, part_id, between):
+        base = unit_at(2 * pack + part_id) * 4
+        slot = lax.rem(pack, 2)
         half = w1.shape[1] // 2
         cuts = [slice(h * half, (h + 1) * half) for h in range(2)]
 
         def first_norm(pair):
-            part = conv_out[slot, pair * breadth : (pair + 1) * breadth, :]
+            begin = (2 * part_id + pair) * breadth
+            part = conv_out[slot, begin : begin + breadth, :]
             spatial = jnp.concatenate([part[:, 0:ch], part[:, ch : 2 * ch]], axis=0) + dw_bias[...]
             return layer_norm(spatial, gain1[...], shift1[...]).astype(BF16)
 
@@ -315,9 +317,9 @@
             for i in range(2):
                 mine = normalized[i * breadth : (i + 1) * breadth]
                 nrm[1 + row + i, 1 : 1 + FAR] = mine.astype(BF16).reshape(FAR, blocks, ch)
-                at = slot * 4 + 2 * pair + i
-                side_out[0, step // 2, pl.ds(at, 1), :] = mine[breadth - 1 : breadth]
-                side_out[1, step // 2, pl.ds(at, 1), :] = mine[0:1]
+                at = part_id * 4 + 2 * pair + i
+                side_out[0, pack, at : at + 1, :] = mine[breadth - 1 : breadth]
+                side_out[1, pack, at : at + 1, :] = mine[0:1]
 
         normed = [first_norm(pair) for pair in range(2)]
         work = [(pair, h) for pair in range(2) for h in range(2)]
@@ -326,8 +328,8 @@
         for k, (pair, h) in enumerate(work):
             if k + 1 < len(work):
                 coming = lift(normed[work[k + 1][0]], cuts[work[k + 1][1]])
-            if between:
-                between[k]()
+            if k % 2 == 0 and between:
+                between[k // 2]()
             hidden[pair].append(twice_gelu(lifted).astype(BF16))
             if k + 1 < len(work):
                 lifted = coming
@@ -370,12 +372,14 @@
     )
     stage_south = remote(nrm.at[1], stage.at[1], stage_send.at[1], stage_recv.at[1], south)
 
-    def step_body(step, carry):
-        @pl.when(step == 2)
+    last = units // 2 - 1
+
+    def pack_body(pack, carry):
+        @pl.when(pack == 1)
         def _():
             ghost_rows()
 
-        @pl.when(step == units - 2)
+        @pl.when(pack == last)
         def _():
             side_finish(1)
             stage_north.start()
@@ -384,12 +388,10 @@
             def _():
                 stage_south.start()
 
-        pointwise(step - 1, [functools.partial(convolve, step, d) for d in range(4)])
-
-        @pl.when(lax.rem(step, 2) == 0)
-        def _():
-            side_start(step // 2 - 1)
-
+        for part in range(2):
+            pieces = [functools.partial(convolve, pack, 2 * part + d) for d in range(2)]
+            pointwise(pack - 1, part, pieces)
+        side_start(pack - 1)
         return carry
 
     for d in range(4):
@@ -397,9 +399,9 @@
     for k in range(len(sources)):
         if k not in first_loads and k < 13:
             loads[k].wait()
-    lax.fori_loop(1, units, step_body, 0)
-    pointwise(units - 1, [])
-    last = units // 2 - 1
+    lax.fori_loop(1, last + 1, pack_body, 0)
+    for part in range(2):
+        pointwise(last, part, [])
     side_start(last)
     loads[13].wait()
     loads[14].wait()
@@ -532,7 +534,7 @@
             pltpu.VMEM((rim, breadth + 2 * FAR, ch), F32),
             pltpu.VMEM((height + 2 * rim, n_off, blocks, ch), BF16),
             pltpu.VMEM((4 * ks * 2 * ch, 2 * ch), BF16),
-            pltpu.VMEM((2, 2 * breadth, 2 * ch), F32),
+            pltpu.VMEM((2, 4 * breadth, 2 * ch), F32),
             pltpu.VMEM((height + 2, FAR + 2, blocks, ch), BF16),
             pltpu.VMEM((2, packs, 8, ch), F32),
             pltpu.VMEM((2, packs, 8, ch), F32),
@@ -551,7 +553,7 @@
             dma((len(arrays),)),
         ],
         compiler_params=pltpu.CompilerParams(
-            collective_id=0, has_side_effects=True, vmem_limit_bytes=40 * 1024 * 1024
+            collective_id=0, has_side_effects=True, vmem_limit_bytes=56 * 1024 * 1024
         ),
     )(*arrays)
 

time: 43.4 us -> 41.7 us (0.961)
  local copies, waits for them, and re-layouts: 11.1 us -> 1.88 us
  Pallas kernels: 31.5 us -> 39.2 us
    unnamed x31 -> x1, local copies, waits for them, and re-layouts: 11.1 us -> 1.88 us
    pallas_call x1, Pallas kernels: 31.5 us -> 39.2 us  [local(): pl.pallas_call(body, out_shape=jax.ShapeDtypeStruct((height // 2, breadth...]
where the time goes in v4:
time: 41.7 us; the launch traced here: 41.1 us
  Pallas kernels  39.2 us (94%)
  local copies, waits for them, and re-layouts  1.88 us (5%)
    pallas_call x1, Pallas kernels, local(): pl.pallas_call(body, out_shape=jax.ShapeDtypeStruct((height // 2, breadth...  39.2 us
    unnamed x1, local copies, waits for them, and re-layouts  1.88 us

profile of v4, /device:TPU:0, one launch (start us, length us, event | category | flops | bytes accessed | tf_op | source)
XLA Modules:
  0.0 41.1 jit_solution(3366515627721528730)
XLA Ops:
  0.0 39.2 %shard_map.145 = bf16[16,64,256]{2,1,0:T(8,128)(2,1)} custom-call(bf16[32,128,128]{2,1,0:T(8,128)(2,1)} %refs_0_.1, s32[32,128]{1,0:T(8,128)} %refs_1_.1, f32[7,7,128]{2,1,0:T(8,128)} %refs_2_.1, f32[1,128]{1,0:T(1,128)} %bitcast.13, f32[1,128]{1,0:T(1,128)} %bitcast.14, f32[1,128]{1,0:T(1,128)} %bitcast.15, bf16[128,512]{1,0:T(8,128)(2,1)} %refs_6_.1, ...), custom_call_target="tpu_custom_call" | custom-call | tf_op jit(solution)/shard_map/pallas_call | solution.py:523
  39.2 1.9 %copy.17 = bf16[16,64,256]{2,1,0:T(8,128)(2,1)} copy(bf16[16,64,256]{2,1,0:T(8,128)(2,1)} %shard_map.145) | data formatting | bytes 1048576
